TPU v7x, 256 devices: a whole 4x4x8 slice. The times are simulated.
256 devices in a mesh: section: 16 (over z_hi, x, core), tensor: 16 (over y, z_lo).
Axes of the slice: x: 4, y: 4, z: 8 (z_hi: 2, z_lo: 4; z = z_hi * 4 + z_lo), core: 2. Of those that a mesh axis runs over, the one named last changes fastest.
Arguments:
- hidden: bfloat16 [256, 16384], P('section', 'tensor'), as said below
- head_weight: bfloat16 [45056, 16384], P(('section', 'tensor')), as said below
- targets: int32 [256], replicated, may hold values from 0 to 45055
- loss_weight: float32 [256], replicated, may hold values from 0.5 to 4
Outputs:
- token_loss: float32 [256], replicated
- grad_weight: bfloat16 [45056, 16384], P(('section', 'tensor'))
- grad_hidden: bfloat16 [256, 16384], P('section', 'tensor')
Inputs may be any that keep to these rules, and one draw needn't show every extreme that they name: hidden entries lie within -16 and 16. head_weight entries lie within -18 / sqrt(16384) and 18 / sqrt(16384).
All inputs are finite; a program needn't handle non-finite values.
Results may differ from a plain program's by a relative error of at most 0.0046.
Values may be sent and summed in bfloat16 or wider, within the bound.
A program may use at most 128 MiB of HBM per device.

v0:
```python
import jax
import jax.numpy as jnp
from jax import lax
from jax.sharding import PartitionSpec as P


def global_stats(shard_logits, shard_hit):
    picked_local = jnp.sum(jnp.where(shard_hit, shard_logits, jnp.float32(0.0)), axis=1)
    row_top = lax.pmax(jnp.max(shard_logits, axis=1), ("section", "tensor"))
    row_total, picked = lax.psum(
        (jnp.sum(jnp.exp(shard_logits - row_top[:, None]), axis=1), picked_local),
        ("section", "tensor"),
    )
    lse = row_top + jnp.log(row_total)
    return (lse, lse - picked)


def on_device(hidden, head_weight, targets, loss_weight):
    shard_len = head_weight.shape[0]
    groups = lax.axis_size("tensor")
    section_idx = lax.axis_index("section")
    tensor_idx = lax.axis_index("tensor")
    features = lax.all_gather(hidden, "tensor", axis=1, tiled=True)
    rows_all = lax.all_gather(features, "section", axis=0, tiled=True)
    logits = lax.dot_general(
        rows_all, head_weight, (((1,), (1,)), ((), ())), preferred_element_type=jnp.float32
    )
    offset = (section_idx * groups + tensor_idx) * shard_len
    columns = offset + jnp.arange(shard_len, dtype=jnp.int32)
    hit = columns[None, :] == targets[:, None]
    lse, token_loss = global_stats(logits, hit)
    dlogits = (
        loss_weight[:, None] * (jnp.exp(logits - lse[:, None]) - hit.astype(jnp.float32))
    ).astype(jnp.bfloat16)
    grad_weight = lax.dot_general(
        dlogits, rows_all, (((0,), (0,)), ((), ())), preferred_element_type=jnp.float32
    ).astype(jnp.bfloat16)
    partial_sums = jnp.dot(dlogits, head_weight, preferred_element_type=jnp.float32)
    by_feature = lax.psum_scatter(partial_sums, "tensor", scatter_dimension=1, tiled=True)
    summed = lax.psum_scatter(by_feature, "section", scatter_dimension=0, tiled=True)
    return (token_loss, grad_weight, summed.astype(jnp.bfloat16))


def solution(mesh):
    in_specs = (P("section", "tensor"), P(("section", "tensor"), None), P(), P())
    out_specs = (P(), P(("section", "tensor"), None), P("section", "tensor"))
    return jax.shard_map(
        on_device, mesh=mesh, in_specs=in_specs, out_specs=out_specs, check_vma=False
    )
```

profile of v0, /device:TPU:1, one launch (start us, length us, event | category | flops | bytes accessed | tf_op | source)
XLA Modules:
  0.0 773.3 jit_solution(8836942060031227028)
XLA Ops:
  7.2 0.0 all-gather.2.cloned.1.call-start
  7.2 44.6 %all_gather.6 = bf16[16,16384]{1,0:T(8,128)(2,1)} all-gather(bf16[16,1024]{1,0:T(8,128)(2,1)} %param.4), channel_id=1, replica_groups=mesh['section'=16,'tensor'=16] {'tensor'}, dimensions={1}, use_global_device_ids=true | all-gather | bytes 557056 | tf_op jit(solution)/shard_map/all_gather | solution.py:23
  51.8 0.0 all-gather.2.cloned.1.call-update
  51.8 0.0 reduce-scatter.3.cloned.1.call-start
  51.9 0.0 copy-start
  51.9 0.0 copy-start.1
  51.9 113.8 %all-gather.2.cloned.1.call-done = bf16[256,16384]{1,0:T(8,128)(2,1)} async-done(((bf16[16,16384]{1,0:T(8,128)(2,1)}), bf16[256,16384]{1,0:T(8,128)(2,1)}) %all-gather.2.cloned.1.call-update) | async-done | bytes 8388624 | tf_op jit(solution)/shard_map/all_gather | solution.py:24
  165.7 8.0 %fusion.8 = (f32[256]{0:T(256)S(1)}, f32[256,176]{0,1:T(8,128)S(1)}) fusion(bf16[256,16384]{1,0:T(8,128)(2,1)} %all-gather.2.cloned.1.call-done, bf16[176,16384]{1,0:T(8,128)(2,1)} %param.5), kind=kOutput, calls=%fused_computation.12 | convolution fusion | flops 1476439808 | bytes 14337024 | tf_op jit(solution)/shard_map/dot_general | solution.py:25
  173.7 73.8 %pmax.7 = f32[256]{0:T(256)S(1)} all-reduce(f32[256]{0:T(256)S(1)} %get-tuple-element.9), channel_id=1, replica_groups=mesh['section'=16,'tensor'=16] {'section','tensor'}, use_global_device_ids=true, to_apply=%region_1.2 | all-reduce | flops 256 | bytes 2048 | tf_op jit(solution)/shard_map/pmax | solution.py:9
  247.5 0.0 copy-done
  247.5 0.1 fusion
  247.6 74.3 %all-reduce = (f32[256]{0:T(256)S(1)}, f32[256]{0:T(256)S(1)}) all-reduce(f32[256]{0:T(256)S(1)} %get-tuple-element.4, f32[256]{0:T(256)S(1)} %get-tuple-element.3), channel_id=1, replica_groups=mesh['section'=16,'tensor'=16] {'section','tensor'}, use_global_device_ids=true, to_apply=%region_3.4 | all-reduce | flops 512 | bytes 4096 | tf_op jit(solution)/shard_map/psum | solution.py:10
  321.8 0.6 fusion.7
  322.4 0.0 copy-done.1
  322.4 10.8 %fusion.4 = f32[256,16384]{1,0:T(8,128)} fusion(bf16[176,16384]{1,0:T(8,128)(2,1)} %param.5, f32[256,176]{0,1:T(8,128)S(1)} %get-tuple-element.10, f32[256]{0:T(256)S(1)} %get-tuple-element.8, f32[256]{0:T(256)S(1)} %copy-done.1, s32[256]{0:T(256)S(1)} %copy-done, s32[176]{0:T(256)S(1)} %iota_add_fusion), kind=kOutput, calls=%fused_computation.10 | convolution fusion | flops 1476665344 | bytes 22728384 | tf_op jit(solution)/shard_map/dot_general | solution.py:38
  333.2 0.0 reduce-scatter.3.cloned.1.call-update
  333.2 0.0 reduce-scatter.5.cloned.1.call-start
  333.3 350.8 %reduce-scatter.3.cloned.1.call-done = f32[256,1024]{1,0:T(8,128)} async-done(((f32[256,16384]{1,0:T(8,128)}), f32[256,1024]{1,0:T(8,128)}) %reduce-scatter.3.cloned.1.call-update) | async-done | bytes 1048592 | tf_op jit(solution)/shard_map/reduce_scatter | solution.py:39
  684.1 0.0 reduce-scatter.5.cloned.1.call-update
  684.1 7.6 convolution_convert_fusion
  691.7 73.6 %reduce-scatter.5.cloned.1.call-done = f32[16,1024]{1,0:T(8,128)} async-done(((f32[256,1024]{1,0:T(8,128)}), f32[16,1024]{1,0:T(8,128)}) %reduce-scatter.5.cloned.1.call-update) | async-done | bytes 65552 | tf_op jit(solution)/shard_map/reduce_scatter | solution.py:40
  765.3 1.5 convert_element_type.15
  (1 shorter events, 0.0 us)
Async XLA Ops:
  7.2 158.6 %all-gather.2.cloned.1.call-start = ((), (), s32[]{:S(2)}) async-start(), calls=%async_computation.2 | async-start | bytes 8912896 | tf_op jit(solution)/shard_map/all_gather | solution.py:24
  51.8 632.3 %reduce-scatter.3.cloned.1.call-start = ((), (), s32[]{:S(2)}) async-start(), calls=%async_computation.3 | async-start | bytes 17825792 | tf_op jit(solution)/shard_map/reduce_scatter | solution.py:39
  51.9 195.6 %copy-start = (s32[256]{0:T(256)S(1)}, s32[256]{0:T(256)}, u32[]{:S(2)}) copy-start(s32[256]{0:T(256)} %param.6) | copy-start | bytes 3076
  51.9 270.5 %copy-start.1 = (f32[256]{0:T(256)S(1)}, f32[256]{0:T(256)}, u32[]{:S(2)}) copy-start(f32[256]{0:T(256)} %param.7) | copy-start | bytes 3076
  333.2 432.1 %reduce-scatter.5.cloned.1.call-start = ((), (), s32[]{:S(2)}) async-start(), calls=%async_computation.4 | async-start | bytes 1114112 | tf_op jit(solution)/shard_map/reduce_scatter | solution.py:40
Sparse Core Ops, SparseCore 0:
  51.9 113.7 all-gather.1
  333.3 350.6 reduce-scatter.2
  688.2 77.1 reduce-scatter.4
where the time goes:
time: 775 us; the launch traced here: 773 us
  waiting for transfers between devices  538 us (69%)
  blocking collectives  193 us (25%)
  matrix products  26.4 us (3%)
  between operations  13.8 us (2%)
    reduce_scatter x1, waiting for transfers between devices, on_device(): lax.psum_scatter(partial_sums, 'tensor', scatter_dimension=1, tiled=True)  351 us
    all_gather x1, waiting for transfers between devices, on_device(): rows_all = lax.all_gather(features, 'section', axis=0, tiled=True)  114 us
    psum x1, blocking collectives, global_stats(): lax.psum((jnp.sum(jnp.exp(shard_logits - row_top[:, None]), axis=1), pick...  74.3 us
    pmax x1, blocking collectives, global_stats(): row_top = lax.pmax(jnp.max(shard_logits, axis=1), ('section', 'tensor'))  73.8 us
    reduce_scatter x1, waiting for transfers between devices, on_device(): lax.psum_scatter(by_feature, 'section', scatter_dimension=0, tiled=True)  73.6 us
    all_gather x1, blocking collectives, on_device(): features = lax.all_gather(hidden, 'tensor', axis=1, tiled=True)  44.6 us
  transfers between devices with their start and end apart: 3, of which 3 were waited for; matrix products, arithmetic and copies ran while one was open for 1% of the time, Pallas kernels for 0%

commit v1 on v0

v1 whole, which is shorter than its diff:
```python
import jax
import jax.numpy as jnp
from jax import lax
from jax.experimental import pallas as pl
from jax.experimental.pallas import tpu as pltpu
from jax.sharding import PartitionSpec as P

MESH = pl.DeviceIdType.MESH
F32, BF16 = jnp.float32, jnp.bfloat16
SIZE = {"x": 4, "y": 4, "z": 8, "a": 4, "b": 4}
ZH, ZL = 2, 4
NB = SIZE["y"] * ZL
NQ = ZH * SIZE["x"]
ROWS = 16
FULL, HALF = 1024, 512
STREAMS = (
    (("z", "b", "a"), 0, 256),
    (("z", "a", "b"), 256, 128),
    (("y", "x", "z"), 384, 128),
)
NS = len(STREAMS)
WIDE = {"z": (0, 384), "y": (384, 128)}
LONG = [i for i in range(NS) if STREAMS[i][0][2] == "z"]
SHORT = [i for i in range(NS) if i not in LONG]
BLOCKS = 4


def lead(order):
    f, m, l = (SIZE[a] for a in order)
    return (l, m, f)


def hops(order, p):
    return SIZE[order[p]] // 2


class Kernel:
    def __init__(self, shard, refs):
        self.shard = shard
        self.__dict__.update(refs)
        sec, ten = lax.axis_index("section"), lax.axis_index("tensor")
        self.core = lax.rem(sec, 2)
        z = (sec // 8) * 4 + lax.rem(ten, 4)
        x, y = lax.rem(sec // 2, 4), ten // 4
        self.me = {"x": x, "y": y, "z": z} | self.roles(x, y)
        self.vocab0 = ((sec - self.core) * 16 + ten) * shard
        self.sends = []

    def roles(self, x, y):
        return {"a": jnp.where(self.core == 0, y, x), "b": jnp.where(self.core == 0, x, y)}

    def dev(self, core=None, **move):
        c = dict(self.me)
        for a, d in move.items():
            c[a] = lax.rem(c[a] + d + SIZE[a], SIZE[a])
            if a in ("a", "b"):
                first = self.core == (0 if a == "b" else 1)
                c["x"], c["y"] = jnp.where(first, c[a], c["x"]), jnp.where(first, c["y"], c[a])
        core = self.core if core is None else core
        return ((c["z"] // 4) * 8 + c["x"] * 2 + core, c["y"] * 4 + lax.rem(c["z"], 4))

    def remote(self, src, dst, ssem, rsem, device):
        return pltpu.make_async_remote_copy(
            src_ref=src, dst_ref=dst, send_sem=ssem, recv_sem=rsem, device_id=device, device_id_type=MESH
        )

    def send(self, *args):
        copy = self.remote(*args)
        copy.start()
        self.sends.append(copy)
        return copy

    def spread_copy(self, a, r, d):
        n = SIZE[a]
        col, width = WIDE[a]
        other = 1 - self.core
        to_core = other if r else self.core
        src = self.hid.at[:, pl.ds(pl.multiple_of(to_core * HALF + col, 128), width)]
        buf, sem = self.first[a], self.first_sem[a]
        if r == 0 and d == 0:
            return pltpu.make_async_copy(src, buf.at[self.core, self.me[a]], sem.at[1, 0, 0]), None
        dev = self.dev(core=to_core, **{a: d})
        sems = (sem.at[0, r, d], sem.at[1, r, d], dev)
        got = buf.at[to_core, lax.rem(self.me[a] - d + n, n)]
        return self.remote(src, buf.at[self.core, self.me[a]], *sems), self.remote(src, got, *sems)

    def spread(self):
        for a in ("z", "y"):
            for d in range(SIZE[a]):
                for r in (0, 1):
                    if d or r:
                        copy, _ = self.spread_copy(a, r, d)
                        copy.start()
                        self.sends.append(copy)

    def spread_wait(self):
        for a in ("z", "y"):
            for d in range(SIZE[a]):
                for r in (0, 1):
                    local, got = self.spread_copy(a, r, d)
                    if got is None:
                        local.wait()
                    else:
                        got.wait_recv()

    def gather_copy(self, i, p, way, kind, hop):
        order = STREAMS[i][0]
        a = order[p]
        n, w = SIZE[a], SIZE[order[p - 1]] // 2
        sign = 1 - 2 * way
        half = way if kind == 0 else 1 - way
        idx = (self.me[order[2]],) if p == 1 else ()
        out = lax.rem(self.me[a] - sign * (hop - 1) + n, n)
        got = lax.rem(self.me[a] - sign * hop + n, n)
        tail = (pl.ds(half * w, w),)
        b = self.buf[i]
        sems = (self.ag_send.at[i, p - 1, way, kind, hop - 1], self.ag_recv.at[i, p - 1, way, kind, hop - 1])
        dev = self.dev(**{a: sign})
        src, dst = b.at[idx + (out,) + tail], b.at[idx + (got,) + tail]
        return (src, src) + sems + (dev,), (dst, dst) + sems + (dev,)

    def gather_event(self, i, p, s):
        h = hops(STREAMS[i][0], p)
        ways = [(kind, way) for kind in (0, 1) for way in (0, 1)]
        if s == h:
            for kind, way in ways:
                self.remote(*self.gather_copy(i, p, way, kind, h - kind)[1]).wait_recv()
            return
        for kind, way in ways:
            if s == 0:
                self.send(*self.gather_copy(i, p, way, kind, 1)[0])
            elif s < h - kind:
                self.remote(*self.gather_copy(i, p, way, kind, s)[1]).wait_recv()
                self.send(*self.gather_copy(i, p, way, kind, s + 1)[0])

    def reduce_copy(self, i, p, way, kind, hop):
        order = STREAMS[i][0]
        w = SIZE[order[p - 1]] // 2
        half = way if kind == 0 else 1 - way
        at = (way, hop - 1, pl.ds(half * w, w))
        return (
            self.rs_out[i][p].at[at],
            self.rs_in[i][p].at[at],
            self.rs_send.at[i, p - 1, way, kind, hop - 1],
            self.rs_recv.at[i, p - 1, way, kind, hop - 1],
            self.dev(**{order[p]: 1 - 2 * way}),
        )

    def over(self, p, lo, size, body):
        if p == 2:
            for r in range(lo, lo + size):
                body((r,))
        else:
            body((pl.ds(lo, size),))

    def reduce_event(self, i, p, s):
        order = STREAMS[i][0]
        a = order[p]
        n, w, h = SIZE[a], SIZE[order[p - 1]] // 2, hops(order, p)
        part, out, got = self.part[i], self.rs_out[i][p], self.rs_in[i][p]
        base = (self.me[order[2]],) if p == 1 else ()
        ways = [(kind, way) for kind in (0, 1) for way in (0, 1)]
        if s == h:
            for kind, way in ways:
                self.remote(*self.reduce_copy(i, p, way, kind, h - kind)).wait_recv()
            mine = base + (self.me[a],)
            for half in (0, 1):
                far, near = (half, h - 1), (1 - half, h - 2)

                def add(r):
                    part[mine + r] = part[mine + r] + (got[far + r].astype(F32) + got[near + r].astype(F32))

                self.over(p, half * w, w, add)
            return
        for kind, way in ways:
            if s and s >= h - kind:
                continue
            if s:
                self.remote(*self.reduce_copy(i, p, way, kind, s)).wait_recv()
            half = way if kind == 0 else 1 - way
            d = h - kind - s
            idx = base + (lax.rem(self.me[a] + (1 - 2 * way) * d + n, n),)

            def put(r):
                v = part[idx + r]
                if s:
                    v = v + got[(way, s - 1) + r].astype(F32)
                out[(way, s) + r] = v.astype(BF16)

            self.over(p, half * w, w, put)
            self.send(*self.reduce_copy(i, p, way, kind, s + 1))

    def collect_copy(self, g, a, d):
        n = SIZE[a]
        to = lax.rem(self.me[a] + d, n)
        sems = self.last_sem[a]
        return self.remote(
            self.last_out[a].at[g, to],
            self.last_in[a].at[self.me[a], self.core],
            sems.at[0, g, d],
            sems.at[1, self.core, d],
            self.dev(core=g, **{a: d}),
        )

    def collect_send(self, g, a):
        col = WIDE[a][0]
        out = self.last_out[a]
        for i in range(NS):
            order, off, width = STREAMS[i]
            if order[0] == a:
                mine = self.part[i].at[self.me[order[2]], self.me[order[1]]]
                out[g, :, :, off - col : off - col + width] = mine[:, g * ROWS : (g + 1) * ROWS]

        for d in range(SIZE[a]):
            copy = self.collect_copy(g, a, d)
            if d:
                copy.start()
                self.sends.append(copy)
            else:

                @pl.when(self.core != g)
                def _():
                    copy.start()

                @pl.when(self.core == g)
                def _():
                    self.last_in[a][self.me[a], g] = out[g, self.me[a]]

    def collect_wait(self, g, a):
        n = SIZE[a]
        col, width = WIDE[a]
        sems = self.last_sem[a]
        buf = self.last_in[a]

        @pl.when(self.core == g)
        def _():
            for d in range(n):
                for c in (g, 1 - g):
                    if d or c != g:
                        slot = buf.at[lax.rem(self.me[a] - d + n, n), c]
                        self.remote(
                            slot, slot, sems.at[0, g, d], sems.at[1, c, d], self.dev(core=c, **{a: -d})
                        ).wait_recv()
            for c in (0, 1):
                v = buf[0, c]
                for e in range(1, n):
                    v = v + buf[e, c]
                self.gh[:, c * HALF + col : c * HALF + col + width] = v.astype(BF16)

        @pl.when(self.core != g)
        def _():
            self.collect_copy(g, a, 0).wait_send()

    def piece(self, i, y, zl):
        order, _, _ = STREAMS[i]
        return jnp.concatenate([self.buf[i][self.at(order, x, y, zh * ZL + zl)] for zh in range(ZH) for x in range(4)], axis=0)

    def at(self, order, x, y, z):
        c = {"x": x, "y": y, "z": z} | self.roles(x, y)
        return (c[order[2]], c[order[1]], c[order[0]])

    def hidden_block(self, j):
        y, zl = j // ZL, lax.rem(j, ZL)
        return jnp.concatenate([self.piece(i, y, zl) for i in range(NS)], axis=1)

    def gather(self):
        for i, (order, off, width) in enumerate(STREAMS):
            col = off - WIDE[order[0]][0]
            mine = self.buf[i].at[self.me[order[2]], self.me[order[1]]]
            for g in (0, 1):
                mine[:, g * ROWS : (g + 1) * ROWS] = self.first[order[0]][g, :, :, col : col + width]
            self.gather_event(i, 1, 0)
        for i in range(NS):
            self.gather_event(i, 1, 1)
        for i in LONG + SHORT:
            self.gather_event(i, 1, 2)
            self.gather_event(i, 2, 0)

        @pl.loop(0, NB)
        def _(j):
            self.weight_copies(j)[1].start()

        for streams, s in ((LONG, 1), (SHORT, 1), (LONG, 2), (LONG, 3), (SHORT, 2), (LONG, 4)):
            for i in streams:
                self.gather_event(i, 2, s)

    def drain(self, copies):
        for copy in copies:
            copy.wait_send()

    def reduce(self, meanwhile):
        before, self.sends = self.sends, []
        for i in LONG + SHORT:
            self.reduce_event(i, 2, 0)
        for streams, s in ((LONG, 1), (SHORT, 1), (LONG, 2), (LONG, 3)):
            next(meanwhile, None)
            if streams is SHORT:
                self.drain(before)
            for i in streams:
                self.reduce_event(i, 2, s)
        for i in SHORT:
            self.reduce_event(i, 2, 2)
            self.reduce_event(i, 1, 0)
        for i in LONG:
            self.reduce_event(i, 2, 4)
            self.reduce_event(i, 1, 0)
        for i in SHORT + LONG:
            self.reduce_event(i, 1, 1)
        for i in SHORT:
            self.reduce_event(i, 1, 2)
        for g in (0, 1):
            self.collect_send(g, "z")
        for i in LONG:
            self.reduce_event(i, 1, 2)
        before, self.sends = self.sends, []
        for g in (0, 1):
            self.collect_send(g, "y")
        self.drain(before)
        for g in (0, 1):
            self.collect_wait(g, "z")
        for g in (0, 1):
            self.collect_wait(g, "y")

    def loss_and_grads(self):
        self.wait_weight()
        acc = self.lg
        acc[...] = jnp.zeros_like(acc)

        @pl.loop(0, NB // BLOCKS)
        def _(b):
            js = [b * BLOCKS + e for e in range(BLOCKS)]
            acc[...] += lax.dot_general(
                jnp.concatenate([self.wv[j] for j in js], axis=1),
                jnp.concatenate([self.hidden_block(j) for j in js], axis=1),
                (((1,), (1,)), ((), ())),
                preferred_element_type=F32,
            )

        swap = (acc, self.lg_in, self.lg_sem.at[0], self.lg_sem.at[1], self.dev(core=1 - self.core))
        self.send(*swap)
        target, scale = self.tgt[...].reshape(1, -1), self.lw[...].reshape(1, -1)
        self.remote(*swap).wait_recv()
        logits = acc[...] + self.lg_in[...]
        self.lg_sum[...] = logits
        row = lax.broadcasted_iota(jnp.int32, logits.shape, 0)
        row = row + jnp.where(row < self.shard, self.vocab0, self.vocab0 + 15 * self.shard)
        hit = row == target
        top = jnp.max(logits, axis=0, keepdims=True)
        total = jnp.sum(jnp.exp(logits - top), axis=0, keepdims=True)
        picked = jnp.sum(jnp.where(hit, logits, 0.0), axis=0, keepdims=True)
        merged = self.stats(0, (top, total, picked), [(dx, dy, 0) for dx in range(4) for dy in range(4)])
        top, total, picked = self.stats(1, merged, [(0, 0, dz) for dz in range(8)])
        lse = top + jnp.log(total)
        self.loss[...] = (lse - picked).reshape(2 * NQ * ROWS)
        dl = scale * (jnp.exp(self.lg_sum[...] - lse) - (row == target).astype(F32))
        self.dlt[...] = dl.astype(BF16)
        self.dlr[...] = dl.T.astype(BF16)

        @pl.loop(0, NB, unroll=BLOCKS)
        def _(j):
            y, zl = j // ZL, lax.rem(j, ZL)
            o = jnp.dot(self.dlr[...], self.wv[j], preferred_element_type=F32)
            for i, (order, off, width) in enumerate(STREAMS):
                for zh in range(ZH):
                    for x in range(4):
                        q = (zh * 4 + x) * 2 * ROWS
                        self.part[i][self.at(order, x, y, zh * ZL + zl)] = o[q : q + 2 * ROWS, off : off + width]

    def stats(self, phase, mine, moves):
        buf = (self.st0, self.st1)[phase]
        own = self.me["x"] * 4 + self.me["y"] if phase == 0 else self.me["z"]
        sems = (self.st0_sem, self.st1_sem)[phase]
        pad = jnp.zeros((5, 256), F32)
        buf[own] = jnp.concatenate(mine + (pad,), axis=0)
        for e, (dx, dy, dz) in enumerate(moves):
            if e:
                self.send(buf.at[own], buf.at[own], sems.at[0, e], sems.at[1, e], self.dev(x=dx, y=dy, z=dz))
        for e, (dx, dy, dz) in enumerate(moves):
            if e:
                if phase == 0:
                    src = lax.rem(self.me["x"] - dx + 4, 4) * 4 + lax.rem(self.me["y"] - dy + 4, 4)
                else:
                    src = lax.rem(self.me["z"] - dz + 8, 8)
                self.remote(
                    buf.at[src], buf.at[src], sems.at[0, e], sems.at[1, e], self.dev(x=dx, y=dy, z=dz)
                ).wait_recv()
        tiles = [buf[e] for e in range(len(moves))]
        top = tiles[0][0:1]
        for t in tiles[1:]:
            top = jnp.maximum(top, t[0:1])
        total = picked = jnp.zeros_like(top)
        for t in tiles:
            total = total + t[1:2] * jnp.exp(t[0:1] - top)
            picked = picked + t[2:3]
        return (top, total, picked)

    def weight_copies(self, j):
        c, other = self.core, 1 - self.core
        rows = pl.ds(pl.multiple_of(c * self.shard, 16), self.shard)
        cols = lambda h: pl.ds(pl.multiple_of(j * FULL + h * HALF, HALF), HALF)
        theirs = pl.ds(pl.multiple_of(other * self.shard, 16), self.shard)
        local = pltpu.make_async_copy(self.w.at[:, cols(c)], self.wv.at[j, rows], self.w_sem.at[0, j])
        out = self.remote(
            self.w.at[:, cols(other)], self.wv.at[j, rows], self.w_sem.at[1, j], self.w_sem.at[2, j], self.dev(core=other)
        )
        arrive = self.remote(
            self.w.at[:, cols(other)], self.wv.at[j, theirs], self.w_sem.at[1, j], self.w_sem.at[2, j], self.dev(core=other)
        )
        return local, out, arrive

    def wait_weight(self):
        @pl.loop(0, NB)
        def _(j):
            local, out, arrive = self.weight_copies(j)
            local.wait()
            out.wait_send()
            arrive.wait_recv()

    def grad_copies(self, j):
        c, other = self.core, 1 - self.core
        cols = lambda h: pl.ds(pl.multiple_of(j * FULL + h * HALF, HALF), HALF)
        src = lambda h: self.gwb.at[j, pl.ds(pl.multiple_of(h * self.shard, 16), self.shard)]
        local = pltpu.make_async_copy(src(c), self.gw.at[:, cols(c)], self.g_sem.at[0, j])
        dev = self.dev(core=other)
        out = self.remote(src(other), self.gw.at[:, cols(c)], self.g_sem.at[1, j], self.g_sem.at[2, j], dev)
        arrive = self.remote(src(other), self.gw.at[:, cols(other)], self.g_sem.at[1, j], self.g_sem.at[2, j], dev)
        return local, out, arrive

    def grad_weight(self, lo, hi):
        @pl.loop(lo, hi, unroll=BLOCKS)
        def _(j):
            o = jnp.dot(self.dlt[...], self.hidden_block(j), preferred_element_type=F32)
            self.gwb[j] = o.astype(BF16)
            local, out, _ = self.grad_copies(j)
            local.start()
            out.start()

    def grad_quarters(self):
        for q in range(4):
            self.grad_weight(q * (NB // 4), (q + 1) * (NB // 4))
            yield

    def run(self):
        other = 1 - self.core
        barrier = pltpu.get_barrier_semaphore()
        peers = [dict(x=dx, y=dy) for dx in range(4) for dy in range(4) if dx or dy]
        peers += [dict(z=dz) for dz in range(1, 8)]
        peers += [dict(core=other, z=dz) for dz in range(8)]
        peers += [dict(core=other, y=dy) for dy in range(1, 4)]
        for d in peers:
            pl.semaphore_signal(barrier, inc=1, device_id=self.dev(**d), device_id_type=MESH)
        for a in ("z", "y"):
            self.spread_copy(a, 0, 0)[0].start()

        @pl.loop(0, NB)
        def _(j):
            self.weight_copies(j)[0].start()

        pl.semaphore_wait(barrier, len(peers))
        self.spread()
        self.spread_wait()
        self.gather()
        self.loss_and_grads()
        self.reduce(self.grad_quarters())

        @pl.loop(0, NB)
        def _(j):
            local, out, arrive = self.grad_copies(j)
            local.wait()
            out.wait_send()
            arrive.wait_recv()

        self.drain(self.sends)


def scratch(shard):
    dma = pltpu.SemaphoreType.DMA
    rows = 2 * shard
    out = {
        "wv": pltpu.VMEM((NB, rows, HALF), BF16),
        "lg": pltpu.VMEM((rows, 256), F32),
        "lg_in": pltpu.VMEM((rows, 256), F32),
        "lg_sum": pltpu.VMEM((rows, 256), F32),
        "st0": pltpu.VMEM((16, 8, 256), F32),
        "st1": pltpu.VMEM((8, 8, 256), F32),
        "dlt": pltpu.VMEM((rows, 256), BF16),
        "dlr": pltpu.VMEM((256, rows), BF16),
        "gwb": pltpu.VMEM((NB, rows, HALF), BF16),
        "ag_send": dma((NS, 2, 2, 2, 4)),
        "ag_recv": dma((NS, 2, 2, 2, 4)),
        "rs_send": dma((NS, 2, 2, 2, 4)),
        "rs_recv": dma((NS, 2, 2, 2, 4)),
        "lg_sem": dma((2,)),
        "st0_sem": dma((2, 16)),
        "st1_sem": dma((2, 8)),
        "w_sem": dma((3, NB)),
        "g_sem": dma((3, NB)),
    }
    for a in ("z", "y"):
        n, width = SIZE[a], WIDE[a][1]
        out[f"first{a}"] = pltpu.VMEM((2, n, ROWS, width), BF16)
        out[f"first_sem{a}"] = dma((2, 2, n))
        out[f"last_out{a}"] = pltpu.VMEM((2, n, ROWS, width), F32)
        out[f"last_in{a}"] = pltpu.VMEM((n, 2, ROWS, width), F32)
        out[f"last_sem{a}"] = dma((2, 2, n))
    for i, (order, _, width) in enumerate(STREAMS):
        l, m, f = lead(order)
        out[f"buf{i}"] = pltpu.VMEM((l, m, f, 2 * ROWS, width), BF16)
        out[f"part{i}"] = pltpu.VMEM((l, m, f, 2 * ROWS, width), F32)
        chunk = {2: (m, f, 2 * ROWS, width), 1: (f, 2 * ROWS, width)}
        for p in (1, 2):
            shape = (2, hops(order, p)) + chunk[p]
            out[f"rs_out{i}{p}"] = pltpu.VMEM(shape, BF16)
            out[f"rs_in{i}{p}"] = pltpu.VMEM(shape, BF16)
    return out


def on_device(hidden, head_weight, targets, loss_weight):
    shard, width = head_weight.shape
    spaces = scratch(shard)

    def body(hid, w, tgt, lw, loss, gw, gh, *refs):
        named = dict(zip(spaces, refs))
        args = dict(hid=hid, w=w, tgt=tgt, lw=lw, loss=loss, gw=gw, gh=gh)
        for kind in ("buf", "part"):
            args[kind] = [named.pop(f"{kind}{i}") for i in range(NS)]
        for kind in ("rs_out", "rs_in"):
            args[kind] = [{p: named.pop(f"{kind}{i}{p}") for p in (1, 2)} for i in range(NS)]
        for kind in ("first", "first_sem", "last_out", "last_in", "last_sem"):
            args[kind] = {a: named.pop(f"{kind}{a}") for a in ("z", "y")}
        args.update(named)
        Kernel(shard, args).run()

    vmem, hbm = pl.BlockSpec(memory_space=pltpu.VMEM), pl.BlockSpec(memory_space=pl.ANY)
    loss, gw, gh = pl.pallas_call(
        body,
        out_shape=(
            jax.ShapeDtypeStruct(loss_weight.shape, F32),
            jax.ShapeDtypeStruct((shard, width), BF16),
            jax.ShapeDtypeStruct(hidden.shape, BF16),
        ),
        in_specs=[hbm, hbm, vmem, vmem],
        out_specs=(vmem, hbm, vmem),
        scratch_shapes=list(spaces.values()),
        compiler_params=pltpu.CompilerParams(
            collective_id=0, has_side_effects=True, vmem_limit_bytes=56 * 1024 * 1024
        ),
        cost_estimate=pl.CostEstimate(
            flops=6 * shard * width * 256, bytes_accessed=4 * shard * width, transcendentals=2 * shard * 512
        ),
    )(hidden, head_weight, targets, loss_weight)
    return (loss, gw, gh)


def solution(mesh):
    in_specs = (P("section", "tensor"), P(("section", "tensor"), None), P(), P())
    out_specs = (P(), P(("section", "tensor"), None), P("section", "tensor"))
    return jax.shard_map(
        on_device, mesh=mesh, in_specs=in_specs, out_specs=out_specs, check_vma=False
    )
```

time: 775 us -> 107 us (0.14)
  waiting for transfers between devices: 538 us -> 0 us
  blocking collectives: 193 us -> 0 us
  Pallas kernels: 0 us -> 98.3 us
  matrix products: 26.4 us -> 0 us
  between operations: 13.8 us -> 0.64 us
    reduce_scatter x2 -> x0, waiting for transfers between devices: 424 us -> none  [the longest x1 351 us: on_device(): lax.psum_scatter(partial_sums, 'tensor', scatter_dimension=1, tiled=True)]
    all_gather x1 -> x0, waiting for transfers between devices: 114 us -> none  [on_device(): rows_all = lax.all_gather(features, 'section', axis=0, tiled=True)]
    pallas_call x0 -> x1, Pallas kernels: none -> 98.3 us  [on_device(): pl.pallas_call(body, out_shape=(jax.ShapeDtypeStruct(loss_weight.shape, F...]
    psum x1 -> x0, blocking collectives: 74.3 us -> none  [global_stats(): lax.psum((jnp.sum(jnp.exp(shard_logits - row_top[:, None]), axis=1), pick...]
    pmax x1 -> x0, blocking collectives: 73.8 us -> none  [global_stats(): row_top = lax.pmax(jnp.max(shard_logits, axis=1), ('section', 'tensor'))]
    all_gather x1 -> x0, blocking collectives: 44.6 us -> none  [on_device(): features = lax.all_gather(hidden, 'tensor', axis=1, tiled=True)]
    dot_general x3 -> x0, matrix products: 26.4 us -> none  [the longest x1 10.8 us: on_device(): jnp.dot(dlogits, head_weight, preferred_element_type=jnp.float32)]
  transfers between devices with their start and end apart: 3 -> 0, of which waited for: 3 -> 0; matrix products, arithmetic and copies ran while one was open for 1% -> 0% of each run, Pallas kernels for 0% -> 0%
where the time goes in v1:
time: 107 us
  Pallas kernels  98.3 us (92%)
  local copies, waits for them, and re-layouts  7.59 us (7%)
    pallas_call x1, Pallas kernels, on_device(): pl.pallas_call(body, out_shape=(jax.ShapeDtypeStruct(loss_weight.shape, F...  98.3 us
    unnamed x5, local copies, waits for them, and re-layouts  7.59 us

profile of v1, /device:TPU:1, one launch (start us, length us, event | category | flops | bytes accessed | tf_op | source)
XLA Modules:
  0.0 106.5 jit_solution(15676185567847449553)
XLA Ops:
  0.6 98.3 %shard_map.67 = (f32[256]{0:T(256)}, bf16[176,16384]{1,0:T(8,128)(2,1)}, bf16[16,1024]{1,0:T(8,128)(2,1)}) custom-call(bf16[16,1024]{1,0:T(8,128)(2,1)} %hid.1, bf16[176,16384]{1,0:T(8,128)(2,1)} %w.1, s32[256]{0:T(256)} %tgt.1, f32[256]{0:T(256)} %lw.1), custom_call_target="tpu_custom_call" | custom-call | flops 4429185024 | bytes 11534336 | tf_op jit(solution)/shard_map/pallas_call | solution.py:535
  99.0 1.2 %copy.10 = f32[256]{0:T(256)} copy(f32[256]{0:T(256)} %get-tuple-element.6) | data formatting | bytes 2048
  100.2 0.0 copy-start
  100.2 5.7 %copy.11 = bf16[176,16384]{1,0:T(8,128)(2,1)} copy(bf16[176,16384]{1,0:T(8,128)(2,1)} %get-tuple-element.7) | data formatting | bytes 11534336
  105.9 0.0 copy-done
  105.9 0.6 copy.12
Async XLA Ops:
  100.2 5.7 %copy-start = (bf16[16,1024]{1,0:T(8,128)(2,1)S(1)}, bf16[16,1024]{1,0:T(8,128)(2,1)}, u32[]{:S(2)}) copy-start(bf16[16,1024]{1,0:T(8,128)(2,1)} %get-tuple-element.8) | copy-start | bytes 98308

commit v2 on v1

--- a/solution.py
+++ b/solution.py
@@ -1,3 +1,5 @@
+import math
+
 import jax
 import jax.numpy as jnp
 from jax import lax
@@ -25,6 +27,15 @@
 BLOCKS = 4
 
 
+def flat(ref, idx, count):
+    dims = ref.shape[:-1]
+    start, rows = 0, math.prod(dims[len(idx) :])
+    for e, n in zip(idx, dims):
+        start = start * n + e
+    start = pl.multiple_of(start * rows, 32)
+    return ref.reshape(math.prod(dims), ref.shape[-1]).at[pl.ds(start, count * rows)]
+
+
 def lead(order):
     f, m, l = (SIZE[a] for a in order)
     return (l, m, f)
@@ -112,11 +123,10 @@
         idx = (self.me[order[2]],) if p == 1 else ()
         out = lax.rem(self.me[a] - sign * (hop - 1) + n, n)
         got = lax.rem(self.me[a] - sign * hop + n, n)
-        tail = (pl.ds(half * w, w),)
-        b = self.buf[i]
+        at = half * w
         sems = (self.ag_send.at[i, p - 1, way, kind, hop - 1], self.ag_recv.at[i, p - 1, way, kind, hop - 1])
         dev = self.dev(**{a: sign})
-        src, dst = b.at[idx + (out,) + tail], b.at[idx + (got,) + tail]
+        src, dst = (flat(self.buf[i], idx + (e, at), w) for e in (out, got))
         return (src, src) + sems + (dev,), (dst, dst) + sems + (dev,)
 
     def gather_event(self, i, p, s):
@@ -137,10 +147,10 @@
         order = STREAMS[i][0]
         w = SIZE[order[p - 1]] // 2
         half = way if kind == 0 else 1 - way
-        at = (way, hop - 1, pl.ds(half * w, w))
+        at = (way, hop - 1, half * w)
         return (
-            self.rs_out[i][p].at[at],
-            self.rs_in[i][p].at[at],
+            flat(self.rs_out[i][p], at, w),
+            flat(self.rs_in[i][p], at, w),
             self.rs_send.at[i, p - 1, way, kind, hop - 1],
             self.rs_recv.at[i, p - 1, way, kind, hop - 1],
             self.dev(**{order[p]: 1 - 2 * way}),
@@ -535,12 +545,12 @@
     loss, gw, gh = pl.pallas_call(
         body,
         out_shape=(
-            jax.ShapeDtypeStruct(loss_weight.shape, F32),
-            jax.ShapeDtypeStruct((shard, width), BF16),
-            jax.ShapeDtypeStruct(hidden.shape, BF16),
+            pltpu.VMEM(loss_weight.shape, F32),
+            pltpu.VMEM((shard, width), BF16),
+            pltpu.VMEM(hidden.shape, BF16),
         ),
         in_specs=[hbm, hbm, vmem, vmem],
-        out_specs=(vmem, hbm, vmem),
+        out_specs=(vmem, vmem, vmem),
         scratch_shapes=list(spaces.values()),
         compiler_params=pltpu.CompilerParams(
             collective_id=0, has_side_effects=True, vmem_limit_bytes=56 * 1024 * 1024

time: 107 us -> 102 us (0.953)
  local copies, waits for them, and re-layouts: 7.59 us -> 3.71 us
    unnamed x5 -> x3, local copies, waits for them, and re-layouts: 7.59 us -> 3.71 us
where the time goes in v2:
time: 102 us
  Pallas kernels  97.7 us (96%)
  local copies, waits for them, and re-layouts  3.71 us (4%)
    pallas_call x1, Pallas kernels, on_device(): pl.pallas_call(body, out_shape=(pltpu.VMEM(loss_weight.shape, F32), pltpu...  97.7 us
    unnamed x3, local copies, waits for them, and re-layouts  3.71 us

profile of v2, /device:TPU:1, one launch (start us, length us, event | category | flops | bytes accessed | tf_op | source)
XLA Modules:
  0.0 102.0 jit_solution(8599136529873005359)
XLA Ops:
  0.6 97.7 %shard_map.67 = (f32[256]{0:T(256)S(1)}, bf16[176,16384]{1,0:T(8,128)(2,1)S(1)}, bf16[16,1024]{1,0:T(8,128)(2,1)S(1)}) custom-call(bf16[16,1024]{1,0:T(8,128)(2,1)} %hid.1, bf16[176,16384]{1,0:T(8,128)(2,1)} %w.1, s32[256]{0:T(256)} %tgt.1, f32[256]{0:T(256)} %lw.1), custom_call_target="tpu_custom_call" | custom-call | flops 4429185024 | bytes 11534336 | tf_op jit(solution)/shard_map/pallas_call | solution.py:545
  98.3 0.6 copy.10
  98.9 0.6 copy.12
  99.5 2.5 %copy.11 = bf16[176,16384]{1,0:T(8,128)(2,1)} copy(bf16[176,16384]{1,0:T(8,128)(2,1)S(1)} %get-tuple-element.4) | data formatting | bytes 11534336

commit v3 on v1

--- a/solution.py
+++ b/solution.py
@@ -103,46 +103,50 @@
                     else:
                         got.wait_recv()
 
-    def gather_copy(self, i, p, way, kind, hop):
+    def gather_copy(self, i, p, g, way, kind, hop):
         order = STREAMS[i][0]
         a = order[p]
         n, w = SIZE[a], SIZE[order[p - 1]] // 2
         sign = 1 - 2 * way
         half = way if kind == 0 else 1 - way
-        idx = (self.me[order[2]],) if p == 1 else ()
+        tail = pl.ds(half * w, w)
         out = lax.rem(self.me[a] - sign * (hop - 1) + n, n)
         got = lax.rem(self.me[a] - sign * hop + n, n)
-        tail = (pl.ds(half * w, w),)
-        b = self.buf[i]
-        sems = (self.ag_send.at[i, p - 1, way, kind, hop - 1], self.ag_recv.at[i, p - 1, way, kind, hop - 1])
+        at = (i, 0 if p == 1 else 1 + g, way, kind, hop - 1)
+        sems = (self.ag_send.at[at], self.ag_recv.at[at])
         dev = self.dev(**{a: sign})
-        src, dst = b.at[idx + (out,) + tail], b.at[idx + (got,) + tail]
+        if p == 1:
+            src, dst = (self.buf[i].at[:, self.me[order[2]], e, tail] for e in (out, got))
+        else:
+            src, dst = (self.buf[i].at[g, e, tail] for e in (out, got))
         return (src, src) + sems + (dev,), (dst, dst) + sems + (dev,)
 
-    def gather_event(self, i, p, s):
+    def gather_event(self, i, p, s, g=None):
         h = hops(STREAMS[i][0], p)
         ways = [(kind, way) for kind in (0, 1) for way in (0, 1)]
         if s == h:
             for kind, way in ways:
-                self.remote(*self.gather_copy(i, p, way, kind, h - kind)[1]).wait_recv()
+                self.remote(*self.gather_copy(i, p, g, way, kind, h - kind)[1]).wait_recv()
             return
         for kind, way in ways:
             if s == 0:
-                self.send(*self.gather_copy(i, p, way, kind, 1)[0])
+                self.send(*self.gather_copy(i, p, g, way, kind, 1)[0])
             elif s < h - kind:
-                self.remote(*self.gather_copy(i, p, way, kind, s)[1]).wait_recv()
-                self.send(*self.gather_copy(i, p, way, kind, s + 1)[0])
-
-    def reduce_copy(self, i, p, way, kind, hop):
+                self.remote(*self.gather_copy(i, p, g, way, kind, s)[1]).wait_recv()
+                self.send(*self.gather_copy(i, p, g, way, kind, s + 1)[0])
+
+    def reduce_copy(self, i, p, g, way, kind, hop):
         order = STREAMS[i][0]
         w = SIZE[order[p - 1]] // 2
         half = way if kind == 0 else 1 - way
-        at = (way, hop - 1, pl.ds(half * w, w))
+        tail = pl.ds(half * w, w)
+        at = (way, hop - 1, slice(None), tail) if p == 1 else (g, way, hop - 1, tail)
+        sem = (i, 0 if p == 1 else 1 + g, way, kind, hop - 1)
         return (
             self.rs_out[i][p].at[at],
             self.rs_in[i][p].at[at],
-            self.rs_send.at[i, p - 1, way, kind, hop - 1],
-            self.rs_recv.at[i, p - 1, way, kind, hop - 1],
+            self.rs_send.at[sem],
+            self.rs_recv.at[sem],
             self.dev(**{order[p]: 1 - 2 * way}),
         )
 
@@ -153,19 +157,20 @@
         else:
             body((pl.ds(lo, size),))
 
-    def reduce_event(self, i, p, s):
+    def reduce_event(self, i, p, s, g=None):
         order = STREAMS[i][0]
         a = order[p]
         n, w, h = SIZE[a], SIZE[order[p - 1]] // 2, hops(order, p)
         part, out, got = self.part[i], self.rs_out[i][p], self.rs_in[i][p]
-        base = (self.me[order[2]],) if p == 1 else ()
+        base = (slice(None), self.me[order[2]]) if p == 1 else (g,)
+        slot = (lambda way, e: (way, e, slice(None))) if p == 1 else (lambda way, e: (g, way, e))
         ways = [(kind, way) for kind in (0, 1) for way in (0, 1)]
         if s == h:
             for kind, way in ways:
-                self.remote(*self.reduce_copy(i, p, way, kind, h - kind)).wait_recv()
+                self.remote(*self.reduce_copy(i, p, g, way, kind, h - kind)).wait_recv()
             mine = base + (self.me[a],)
             for half in (0, 1):
-                far, near = (half, h - 1), (1 - half, h - 2)
+                far, near = slot(half, h - 1), slot(1 - half, h - 2)
 
                 def add(r):
                     part[mine + r] = part[mine + r] + (got[far + r].astype(F32) + got[near + r].astype(F32))
@@ -176,7 +181,7 @@
             if s and s >= h - kind:
                 continue
             if s:
-                self.remote(*self.reduce_copy(i, p, way, kind, s)).wait_recv()
+                self.remote(*self.reduce_copy(i, p, g, way, kind, s)).wait_recv()
             half = way if kind == 0 else 1 - way
             d = h - kind - s
             idx = base + (lax.rem(self.me[a] + (1 - 2 * way) * d + n, n),)
@@ -184,11 +189,11 @@
             def put(r):
                 v = part[idx + r]
                 if s:
-                    v = v + got[(way, s - 1) + r].astype(F32)
-                out[(way, s) + r] = v.astype(BF16)
+                    v = v + got[slot(way, s - 1) + r].astype(F32)
+                out[slot(way, s) + r] = v.astype(BF16)
 
             self.over(p, half * w, w, put)
-            self.send(*self.reduce_copy(i, p, way, kind, s + 1))
+            self.send(*self.reduce_copy(i, p, g, way, kind, s + 1))
 
     def collect_copy(self, g, a, d):
         n = SIZE[a]
@@ -208,8 +213,7 @@
         for i in range(NS):
             order, off, width = STREAMS[i]
             if order[0] == a:
-                mine = self.part[i].at[self.me[order[2]], self.me[order[1]]]
-                out[g, :, :, off - col : off - col + width] = mine[:, g * ROWS : (g + 1) * ROWS]
+                out[g, :, :, off - col : off - col + width] = self.part[i][g, self.me[order[2]], self.me[order[1]]]
 
         for d in range(SIZE[a]):
             copy = self.collect_copy(g, a, d)
@@ -251,59 +255,179 @@
         def _():
             self.collect_copy(g, a, 0).wait_send()
 
-    def piece(self, i, y, zl):
-        order, _, _ = STREAMS[i]
-        return jnp.concatenate([self.buf[i][self.at(order, x, y, zh * ZL + zl)] for zh in range(ZH) for x in range(4)], axis=0)
+    def piece(self, i, g, y, zl):
+        order = STREAMS[i][0]
+        return jnp.concatenate(
+            [self.buf[i][(g,) + self.at(order, x, y, zh * ZL + zl)] for zh in range(ZH) for x in range(4)], axis=0
+        )
 
     def at(self, order, x, y, z):
         c = {"x": x, "y": y, "z": z} | self.roles(x, y)
         return (c[order[2]], c[order[1]], c[order[0]])
 
-    def hidden_block(self, j):
+    def hidden_block(self, g, j):
         y, zl = j // ZL, lax.rem(j, ZL)
-        return jnp.concatenate([self.piece(i, y, zl) for i in range(NS)], axis=1)
-
-    def gather(self):
+        return jnp.concatenate([self.piece(i, g, y, zl) for i in range(NS)], axis=1)
+
+    def per_group(self, ref, g):
+        v = ref[...].reshape(1, 2 * NQ * ROWS)
+        return jnp.concatenate([v[:, (2 * q + g) * ROWS : (2 * q + g + 1) * ROWS] for q in range(NQ)], axis=1)
+
+    def logits(self, g):
+        acc = self.lg.at[g]
+        acc[...] = jnp.zeros_like(acc)
+
+        @pl.loop(0, NB // BLOCKS)
+        def _(b):
+            js = [b * BLOCKS + e for e in range(BLOCKS)]
+            acc[...] += lax.dot_general(
+                jnp.concatenate([self.wv[j] for j in js], axis=1),
+                jnp.concatenate([self.hidden_block(g, j) for j in js], axis=1),
+                (((1,), (1,)), ((), ())),
+                preferred_element_type=F32,
+            )
+
+        swap = (acc, self.lg_in.at[g], self.lg_sem.at[0, g], self.lg_sem.at[1, g], self.dev(core=1 - self.core))
+        self.send(*swap)
+        target, scale = self.per_group(self.tgt, g), self.per_group(self.lw, g)
+        yield
+        self.remote(*swap).wait_recv()
+        logits = acc[...] + self.lg_in[g]
+        self.lg_sum[g] = logits
+        row = lax.broadcasted_iota(jnp.int32, logits.shape, 0)
+        row = row + jnp.where(row < self.shard, self.vocab0, self.vocab0 + 15 * self.shard)
+        top = jnp.max(logits, axis=0, keepdims=True)
+        total = jnp.sum(jnp.exp(logits - top), axis=0, keepdims=True)
+        picked = jnp.sum(jnp.where(row == target, logits, 0.0), axis=0, keepdims=True)
+        self.stats_send(g, 0, (top, total, picked))
+        yield
+        self.stats_send(g, 1, self.stats_merge(g, 0))
+        yield
+        top, total, picked = self.stats_merge(g, 1)
+        lse = top + jnp.log(total)
+        self.token_loss[g] = lse - picked
+        row = lax.broadcasted_iota(jnp.int32, logits.shape, 0)
+        row = row + jnp.where(row < self.shard, self.vocab0, self.vocab0 + 15 * self.shard)
+        dl = scale * (jnp.exp(self.lg_sum[g] - lse) - (row == target).astype(F32))
+        self.dlt[:, g * 128 : (g + 1) * 128] = dl.astype(BF16)
+        self.dlr[g] = dl.T.astype(BF16)
+
+        @pl.loop(0, NB, unroll=BLOCKS)
+        def _(j):
+            y, zl = j // ZL, lax.rem(j, ZL)
+            o = jnp.dot(self.dlr[g], self.wv[j], preferred_element_type=F32)
+            for i, (order, off, width) in enumerate(STREAMS):
+                for zh in range(ZH):
+                    for x in range(4):
+                        q = (zh * 4 + x) * ROWS
+                        at = (g,) + self.at(order, x, y, zh * ZL + zl)
+                        self.part[i][at] = o[q : q + ROWS, off : off + width]
+
+    def stats_moves(self, phase):
+        if phase == 0:
+            return [(dx, dy, 0) for dx in range(4) for dy in range(4) if dx or dy]
+        return [(0, 0, dz) for dz in range(1, 8)]
+
+    def stats_send(self, g, phase, mine):
+        buf = (self.st0, self.st1)[phase].at[g]
+        own = self.me["x"] * 4 + self.me["y"] if phase == 0 else self.me["z"]
+        sems = (self.st0_sem, self.st1_sem)[phase]
+        buf[own] = jnp.concatenate(mine + (jnp.zeros((5, 128), F32),), axis=0)
+        for e, (dx, dy, dz) in enumerate(self.stats_moves(phase)):
+            self.send(buf.at[own], buf.at[own], sems.at[0, g, e], sems.at[1, g, e], self.dev(x=dx, y=dy, z=dz))
+
+    def stats_merge(self, g, phase):
+        buf = (self.st0, self.st1)[phase].at[g]
+        sems = (self.st0_sem, self.st1_sem)[phase]
+        moves = self.stats_moves(phase)
+        for e, (dx, dy, dz) in enumerate(moves):
+            if phase == 0:
+                src = lax.rem(self.me["x"] - dx + 4, 4) * 4 + lax.rem(self.me["y"] - dy + 4, 4)
+            else:
+                src = lax.rem(self.me["z"] - dz + 8, 8)
+            self.remote(
+                buf.at[src], buf.at[src], sems.at[0, g, e], sems.at[1, g, e], self.dev(x=dx, y=dy, z=dz)
+            ).wait_recv()
+        tiles = [buf[e] for e in range(len(moves) + 1)]
+        top = tiles[0][0:1]
+        for t in tiles[1:]:
+            top = jnp.maximum(top, t[0:1])
+        total = picked = jnp.zeros_like(top)
+        for t in tiles:
+            total = total + t[1:2] * jnp.exp(t[0:1] - top)
+            picked = picked + t[2:3]
+        return (top, total, picked)
+
+    def drain(self):
+        copies, self.sends = self.sends, []
+        return copies
+
+    def pipeline(self):
+        both = LONG + SHORT
+        ag = lambda streams, s, g: [self.gather_event(i, 2, s, g) for i in streams]
+        rs = lambda streams, s, g: [self.reduce_event(i, 2, s, g) for i in streams]
         for i, (order, off, width) in enumerate(STREAMS):
             col = off - WIDE[order[0]][0]
-            mine = self.buf[i].at[self.me[order[2]], self.me[order[1]]]
             for g in (0, 1):
-                mine[:, g * ROWS : (g + 1) * ROWS] = self.first[order[0]][g, :, :, col : col + width]
+                self.buf[i][g, self.me[order[2]], self.me[order[1]]] = self.first[order[0]][g, :, :, col : col + width]
             self.gather_event(i, 1, 0)
         for i in range(NS):
             self.gather_event(i, 1, 1)
-        for i in LONG + SHORT:
+        for i in both:
             self.gather_event(i, 1, 2)
-            self.gather_event(i, 2, 0)
+            self.gather_event(i, 2, 0, 0)
 
         @pl.loop(0, NB)
         def _(j):
             self.weight_copies(j)[1].start()
 
-        for streams, s in ((LONG, 1), (SHORT, 1), (LONG, 2), (LONG, 3), (SHORT, 2), (LONG, 4)):
+        ag(LONG, 1, 0)
+        ag(SHORT, 1, 0)
+        ag(LONG, 2, 0)
+        ag(SHORT, 0, 1)
+        ag(LONG, 3, 0)
+        ag(LONG, 0, 1)
+        ag(SHORT, 2, 0)
+        ag(LONG, 4, 0)
+        self.wait_weight()
+        zero, one, grads = self.logits(0), self.logits(1), self.grad_quarters()
+        next(zero)
+        ag(LONG, 1, 1)
+        ag(SHORT, 1, 1)
+        next(zero)
+        ag(LONG, 2, 1)
+        next(zero)
+        ag(LONG, 3, 1)
+        next(zero, None)
+        rs(both, 0, 0)
+        ag(SHORT, 2, 1)
+        ag(LONG, 4, 1)
+        next(one)
+        rs(LONG, 1, 0)
+        rs(SHORT, 1, 0)
+        next(one)
+        rs(LONG, 2, 0)
+        next(one)
+        rs(LONG, 3, 0)
+        next(one, None)
+        early = self.drain()
+        rs(both, 0, 1)
+        next(grads)
+        rs(SHORT, 2, 0)
+        rs(LONG, 4, 0)
+        rs(LONG, 1, 1)
+        next(grads)
+        rs(SHORT, 1, 1)
+        next(grads)
+        rs(LONG, 2, 1)
+        next(grads)
+        rs(LONG, 3, 1)
+        for copy in early:
+            copy.wait_send()
+        for streams, h in ((SHORT, 2), (LONG, 4)):
             for i in streams:
-                self.gather_event(i, 2, s)
-
-    def drain(self, copies):
-        for copy in copies:
-            copy.wait_send()
-
-    def reduce(self, meanwhile):
-        before, self.sends = self.sends, []
-        for i in LONG + SHORT:
-            self.reduce_event(i, 2, 0)
-        for streams, s in ((LONG, 1), (SHORT, 1), (LONG, 2), (LONG, 3)):
-            next(meanwhile, None)
-            if streams is SHORT:
-                self.drain(before)
-            for i in streams:
-                self.reduce_event(i, 2, s)
-        for i in SHORT:
-            self.reduce_event(i, 2, 2)
-            self.reduce_event(i, 1, 0)
-        for i in LONG:
-            self.reduce_event(i, 2, 4)
-            self.reduce_event(i, 1, 0)
+                self.reduce_event(i, 2, h, 1)
+                self.reduce_event(i, 1, 0)
         for i in SHORT + LONG:
             self.reduce_event(i, 1, 1)
         for i in SHORT:
@@ -312,87 +436,15 @@
             self.collect_send(g, "z")
         for i in LONG:
             self.reduce_event(i, 1, 2)
-        before, self.sends = self.sends, []
         for g in (0, 1):
             self.collect_send(g, "y")
-        self.drain(before)
-        for g in (0, 1):
-            self.collect_wait(g, "z")
-        for g in (0, 1):
-            self.collect_wait(g, "y")
-
-    def loss_and_grads(self):
-        self.wait_weight()
-        acc = self.lg
-        acc[...] = jnp.zeros_like(acc)
-
-        @pl.loop(0, NB // BLOCKS)
-        def _(b):
-            js = [b * BLOCKS + e for e in range(BLOCKS)]
-            acc[...] += lax.dot_general(
-                jnp.concatenate([self.wv[j] for j in js], axis=1),
-                jnp.concatenate([self.hidden_block(j) for j in js], axis=1),
-                (((1,), (1,)), ((), ())),
-                preferred_element_type=F32,
-            )
-
-        swap = (acc, self.lg_in, self.lg_sem.at[0], self.lg_sem.at[1], self.dev(core=1 - self.core))
-        self.send(*swap)
-        target, scale = self.tgt[...].reshape(1, -1), self.lw[...].reshape(1, -1)
-        self.remote(*swap).wait_recv()
-        logits = acc[...] + self.lg_in[...]
-        self.lg_sum[...] = logits
-        row = lax.broadcasted_iota(jnp.int32, logits.shape, 0)
-        row = row + jnp.where(row < self.shard, self.vocab0, self.vocab0 + 15 * self.shard)
-        hit = row == target
-        top = jnp.max(logits, axis=0, keepdims=True)
-        total = jnp.sum(jnp.exp(logits - top), axis=0, keepdims=True)
-        picked = jnp.sum(jnp.where(hit, logits, 0.0), axis=0, keepdims=True)
-        merged = self.stats(0, (top, total, picked), [(dx, dy, 0) for dx in range(4) for dy in range(4)])
-        top, total, picked = self.stats(1, merged, [(0, 0, dz) for dz in range(8)])
-        lse = top + jnp.log(total)
-        self.loss[...] = (lse - picked).reshape(2 * NQ * ROWS)
-        dl = scale * (jnp.exp(self.lg_sum[...] - lse) - (row == target).astype(F32))
-        self.dlt[...] = dl.astype(BF16)
-        self.dlr[...] = dl.T.astype(BF16)
-
-        @pl.loop(0, NB, unroll=BLOCKS)
-        def _(j):
-            y, zl = j // ZL, lax.rem(j, ZL)
-            o = jnp.dot(self.dlr[...], self.wv[j], preferred_element_type=F32)
-            for i, (order, off, width) in enumerate(STREAMS):
-                for zh in range(ZH):
-                    for x in range(4):
-                        q = (zh * 4 + x) * 2 * ROWS
-                        self.part[i][self.at(order, x, y, zh * ZL + zl)] = o[q : q + 2 * ROWS, off : off + width]
-
-    def stats(self, phase, mine, moves):
-        buf = (self.st0, self.st1)[phase]
-        own = self.me["x"] * 4 + self.me["y"] if phase == 0 else self.me["z"]
-        sems = (self.st0_sem, self.st1_sem)[phase]
-        pad = jnp.zeros((5, 256), F32)
-        buf[own] = jnp.concatenate(mine + (pad,), axis=0)
-        for e, (dx, dy, dz) in enumerate(moves):
-            if e:
-                self.send(buf.at[own], buf.at[own], sems.at[0, e], sems.at[1, e], self.dev(x=dx, y=dy, z=dz))
-        for e, (dx, dy, dz) in enumerate(moves):
-            if e:
-                if phase == 0:
-                    src = lax.rem(self.me["x"] - dx + 4, 4) * 4 + lax.rem(self.me["y"] - dy + 4, 4)
-                else:
-                    src = lax.rem(self.me["z"] - dz + 8, 8)
-                self.remote(
-                    buf.at[src], buf.at[src], sems.at[0, e], sems.at[1, e], self.dev(x=dx, y=dy, z=dz)
-                ).wait_recv()
-        tiles = [buf[e] for e in range(len(moves))]
-        top = tiles[0][0:1]
-        for t in tiles[1:]:
-            top = jnp.maximum(top, t[0:1])
-        total = picked = jnp.zeros_like(top)
-        for t in tiles:
-            total = total + t[1:2] * jnp.exp(t[0:1] - top)
-            picked = picked + t[2:3]
-        return (top, total, picked)
+        rows = [v[:, q * ROWS : (q + 1) * ROWS] for q in range(NQ) for v in self.token_loss]
+        self.loss[...] = jnp.concatenate(rows, axis=1).reshape(2 * NQ * ROWS)
+        for copy in self.drain():
+            copy.wait_send()
+        for a in ("z", "y"):
+            for g in (0, 1):
+                self.collect_wait(g, a)
 
     def weight_copies(self, j):
         c, other = self.core, 1 - self.core
@@ -429,7 +481,8 @@
     def grad_weight(self, lo, hi):
         @pl.loop(lo, hi, unroll=BLOCKS)
         def _(j):
-            o = jnp.dot(self.dlt[...], self.hidden_block(j), preferred_element_type=F32)
+            h = jnp.concatenate([self.hidden_block(0, j), self.hidden_block(1, j)], axis=0)
+            o = jnp.dot(self.dlt[...], h, preferred_element_type=F32)
             self.gwb[j] = o.astype(BF16)
             local, out, _ = self.grad_copies(j)
             local.start()
@@ -459,9 +512,8 @@
         pl.semaphore_wait(barrier, len(peers))
         self.spread()
         self.spread_wait()
-        self.gather()
-        self.loss_and_grads()
-        self.reduce(self.grad_quarters())
+        self.token_loss = [None, None]
+        self.pipeline()
 
         @pl.loop(0, NB)
         def _(j):
@@ -470,29 +522,27 @@
             out.wait_send()
             arrive.wait_recv()
 
-        self.drain(self.sends)
-
 
 def scratch(shard):
     dma = pltpu.SemaphoreType.DMA
     rows = 2 * shard
     out = {
         "wv": pltpu.VMEM((NB, rows, HALF), BF16),
-        "lg": pltpu.VMEM((rows, 256), F32),
-        "lg_in": pltpu.VMEM((rows, 256), F32),
-        "lg_sum": pltpu.VMEM((rows, 256), F32),
-        "st0": pltpu.VMEM((16, 8, 256), F32),
-        "st1": pltpu.VMEM((8, 8, 256), F32),
+        "lg": pltpu.VMEM((2, rows, 128), F32),
+        "lg_in": pltpu.VMEM((2, rows, 128), F32),
+        "lg_sum": pltpu.VMEM((2, rows, 128), F32),
+        "st0": pltpu.VMEM((2, 16, 8, 128), F32),
+        "st1": pltpu.VMEM((2, 8, 8, 128), F32),
         "dlt": pltpu.VMEM((rows, 256), BF16),
-        "dlr": pltpu.VMEM((256, rows), BF16),
+        "dlr": pltpu.VMEM((2, 128, rows), BF16),
         "gwb": pltpu.VMEM((NB, rows, HALF), BF16),
-        "ag_send": dma((NS, 2, 2, 2, 4)),
-        "ag_recv": dma((NS, 2, 2, 2, 4)),
-        "rs_send": dma((NS, 2, 2, 2, 4)),
-        "rs_recv": dma((NS, 2, 2, 2, 4)),
-        "lg_sem": dma((2,)),
-        "st0_sem": dma((2, 16)),
-        "st1_sem": dma((2, 8)),
+        "ag_send": dma((NS, 3, 2, 2, 4)),
+        "ag_recv": dma((NS, 3, 2, 2, 4)),
+        "rs_send": dma((NS, 3, 2, 2, 4)),
+        "rs_recv": dma((NS, 3, 2, 2, 4)),
+        "lg_sem": dma((2, 2)),
+        "st0_sem": dma((2, 2, 15)),
+        "st1_sem": dma((2, 2, 7)),
         "w_sem": dma((3, NB)),
         "g_sem": dma((3, NB)),
     }
@@ -505,13 +555,13 @@
         out[f"last_sem{a}"] = dma((2, 2, n))
     for i, (order, _, width) in enumerate(STREAMS):
         l, m, f = lead(order)
-        out[f"buf{i}"] = pltpu.VMEM((l, m, f, 2 * ROWS, width), BF16)
-        out[f"part{i}"] = pltpu.VMEM((l, m, f, 2 * ROWS, width), F32)
-        chunk = {2: (m, f, 2 * ROWS, width), 1: (f, 2 * ROWS, width)}
+        out[f"buf{i}"] = pltpu.VMEM((2, l, m, f, ROWS, width), BF16)
+        out[f"part{i}"] = pltpu.VMEM((2, l, m, f, ROWS, width), F32)
+        ring = {p: (2, hops(order, p)) for p in (1, 2)}
+        shapes = {1: ring[1] + (2, f, ROWS, width), 2: (2,) + ring[2] + (m, f, ROWS, width)}
         for p in (1, 2):
-            shape = (2, hops(order, p)) + chunk[p]
-            out[f"rs_out{i}{p}"] = pltpu.VMEM(shape, BF16)
-            out[f"rs_in{i}{p}"] = pltpu.VMEM(shape, BF16)
+            out[f"rs_out{i}{p}"] = pltpu.VMEM(shapes[p], BF16)
+            out[f"rs_in{i}{p}"] = pltpu.VMEM(shapes[p], BF16)
     return out
 
 
@@ -535,12 +585,12 @@
     loss, gw, gh = pl.pallas_call(
         body,
         out_shape=(
-            jax.ShapeDtypeStruct(loss_weight.shape, F32),
-            jax.ShapeDtypeStruct((shard, width), BF16),
-            jax.ShapeDtypeStruct(hidden.shape, BF16),
+            pltpu.VMEM(loss_weight.shape, F32),
+            pltpu.VMEM((shard, width), BF16),
+            pltpu.VMEM(hidden.shape, BF16),
         ),
         in_specs=[hbm, hbm, vmem, vmem],
-        out_specs=(vmem, hbm, vmem),
+        out_specs=(vmem, vmem, vmem),
         scratch_shapes=list(spaces.values()),
         compiler_params=pltpu.CompilerParams(
             collective_id=0, has_side_effects=True, vmem_limit_bytes=56 * 1024 * 1024

time: 107 us -> 110 us (1.028)
  Pallas kernels: 98.3 us -> 106 us
  local copies, waits for them, and re-layouts: 7.59 us -> 3.71 us
    pallas_call x1, Pallas kernels: 98.3 us -> 106 us  [on_device(): pl.pallas_call(body, out_shape=(pltpu.VMEM(loss_weight.shape, F32), pltpu...]
    unnamed x5 -> x3, local copies, waits for them, and re-layouts: 7.59 us -> 3.71 us
where the time goes in v3:
time: 110 us
  Pallas kernels  106 us (96%)
  local copies, waits for them, and re-layouts  3.71 us (3%)
    pallas_call x1, Pallas kernels, on_device(): pl.pallas_call(body, out_shape=(pltpu.VMEM(loss_weight.shape, F32), pltpu...  106 us
    unnamed x3, local copies, waits for them, and re-layouts  3.71 us

profile of v3, /device:TPU:1, one launch (start us, length us, event | category | flops | bytes accessed | tf_op | source)
XLA Modules:
  0.0 109.9 jit_solution(17082641869153467849)
XLA Ops:
  0.6 105.6 %shard_map.67 = (f32[256]{0:T(256)S(1)}, bf16[176,16384]{1,0:T(8,128)(2,1)S(1)}, bf16[16,1024]{1,0:T(8,128)(2,1)S(1)}) custom-call(bf16[16,1024]{1,0:T(8,128)(2,1)} %hid.1, bf16[176,16384]{1,0:T(8,128)(2,1)} %w.1, s32[256]{0:T(256)} %tgt.1, f32[256]{0:T(256)} %lw.1), custom_call_target="tpu_custom_call" | custom-call | flops 4429185024 | bytes 11534336 | tf_op jit(solution)/shard_map/pallas_call | solution.py:585
  106.2 0.6 copy.10
  106.8 0.6 copy.12
  107.4 2.5 %copy.11 = bf16[176,16384]{1,0:T(8,128)(2,1)} copy(bf16[176,16384]{1,0:T(8,128)(2,1)S(1)} %get-tuple-element.4) | data formatting | bytes 11534336

commit v4 on v2

--- a/solution.py
+++ b/solution.py
@@ -24,7 +24,7 @@
 WIDE = {"z": (0, 384), "y": (384, 128)}
 LONG = [i for i in range(NS) if STREAMS[i][0][2] == "z"]
 SHORT = [i for i in range(NS) if i not in LONG]
-BLOCKS = 4
+BLOCKS = 2
 
 
 def flat(ref, idx, count):
@@ -55,7 +55,6 @@
         x, y = lax.rem(sec // 2, 4), ten // 4
         self.me = {"x": x, "y": y, "z": z} | self.roles(x, y)
         self.vocab0 = ((sec - self.core) * 16 + ten) * shard
-        self.sends = []
 
     def roles(self, x, y):
         return {"a": jnp.where(self.core == 0, y, x), "b": jnp.where(self.core == 0, x, y)}
@@ -76,43 +75,38 @@
         )
 
     def send(self, *args):
-        copy = self.remote(*args)
-        copy.start()
-        self.sends.append(copy)
-        return copy
-
-    def spread_copy(self, a, r, d):
-        n = SIZE[a]
+        self.remote(*args).start()
+
+    def settle(self, ref, sem):
+        pltpu.make_async_copy(ref, ref, sem).wait()
+
+    def spread_own(self, a):
         col, width = WIDE[a]
-        other = 1 - self.core
-        to_core = other if r else self.core
-        src = self.hid.at[:, pl.ds(pl.multiple_of(to_core * HALF + col, 128), width)]
-        buf, sem = self.first[a], self.first_sem[a]
-        if r == 0 and d == 0:
-            return pltpu.make_async_copy(src, buf.at[self.core, self.me[a]], sem.at[1, 0, 0]), None
-        dev = self.dev(core=to_core, **{a: d})
-        sems = (sem.at[0, r, d], sem.at[1, r, d], dev)
-        got = buf.at[to_core, lax.rem(self.me[a] - d + n, n)]
-        return self.remote(src, buf.at[self.core, self.me[a]], *sems), self.remote(src, got, *sems)
+        src = self.hid.at[:, pl.ds(pl.multiple_of(self.core * HALF + col, 128), width)]
+        return pltpu.make_async_copy(src, self.first[a].at[self.core, self.me[a]], self.first_sem[a].at[1])
 
     def spread(self):
         for a in ("z", "y"):
-            for d in range(SIZE[a]):
-                for r in (0, 1):
-                    if d or r:
-                        copy, _ = self.spread_copy(a, r, d)
-                        copy.start()
-                        self.sends.append(copy)
+            n = SIZE[a]
+            col, width = WIDE[a]
+
+            @pl.loop(1, 2 * n)
+            def _(e):
+                to_core = lax.rem(self.core + e, 2)
+                src = self.hid.at[:, pl.ds(pl.multiple_of(to_core * HALF + col, 128), width)]
+                dst = self.first[a].at[self.core, self.me[a]]
+                dev = self.dev(core=to_core, **{a: e // 2})
+                self.send(src, dst, self.first_sem[a].at[0], self.first_sem[a].at[1], dev)
+
+    def first_flat(self, a):
+        return self.first[a].reshape(2 * SIZE[a], ROWS, WIDE[a][1])
 
     def spread_wait(self):
         for a in ("z", "y"):
-            for d in range(SIZE[a]):
-                for r in (0, 1):
-                    local, got = self.spread_copy(a, r, d)
-                    if got is None:
-                        local.wait()
-                    else:
-                        got.wait_recv()
+            self.settle(self.first[a], self.first_sem[a].at[1])
+
+    def settle_all(self, ref, sem, count):
+        self.settle(ref.at[pl.ds(0, count)], sem)
 
     def gather_copy(self, i, p, way, kind, hop):
         order = STREAMS[i][0]
@@ -124,7 +118,7 @@
         out = lax.rem(self.me[a] - sign * (hop - 1) + n, n)
         got = lax.rem(self.me[a] - sign * hop + n, n)
         at = half * w
-        sems = (self.ag_send.at[i, p - 1, way, kind, hop - 1], self.ag_recv.at[i, p - 1, way, kind, hop - 1])
+        sems = (self.ag_send.at[i, p - 1], self.ag_recv.at[i, p - 1, way, kind, hop - 1])
         dev = self.dev(**{a: sign})
         src, dst = (flat(self.buf[i], idx + (e, at), w) for e in (out, got))
         return (src, src) + sems + (dev,), (dst, dst) + sems + (dev,)
@@ -151,7 +145,7 @@
         return (
             flat(self.rs_out[i][p], at, w),
             flat(self.rs_in[i][p], at, w),
-            self.rs_send.at[i, p - 1, way, kind, hop - 1],
+            self.rs_send.at[i, p - 1],
             self.rs_recv.at[i, p - 1, way, kind, hop - 1],
             self.dev(**{order[p]: 1 - 2 * way}),
         )
@@ -201,16 +195,10 @@
             self.send(*self.reduce_copy(i, p, way, kind, s + 1))
 
     def collect_copy(self, g, a, d):
-        n = SIZE[a]
-        to = lax.rem(self.me[a] + d, n)
-        sems = self.last_sem[a]
-        return self.remote(
-            self.last_out[a].at[g, to],
-            self.last_in[a].at[self.me[a], self.core],
-            sems.at[0, g, d],
-            sems.at[1, self.core, d],
-            self.dev(core=g, **{a: d}),
-        )
+        to = lax.rem(self.me[a] + d, SIZE[a])
+        sem = self.last_sem[a]
+        slot = self.last_in[a].at[self.me[a] * 2 + self.core]
+        return self.remote(self.last_out[a].at[g, to], slot, sem.at[0, g], sem.at[1, 0], self.dev(core=g, **{a: d}))
 
     def collect_send(self, g, a):
         col = WIDE[a][0]
@@ -221,45 +209,37 @@
                 mine = self.part[i].at[self.me[order[2]], self.me[order[1]]]
                 out[g, :, :, off - col : off - col + width] = mine[:, g * ROWS : (g + 1) * ROWS]
 
-        for d in range(SIZE[a]):
-            copy = self.collect_copy(g, a, d)
-            if d:
-                copy.start()
-                self.sends.append(copy)
-            else:
-
-                @pl.when(self.core != g)
-                def _():
-                    copy.start()
-
-                @pl.when(self.core == g)
-                def _():
-                    self.last_in[a][self.me[a], g] = out[g, self.me[a]]
+        @pl.loop(1, SIZE[a])
+        def _(d):
+            self.collect_copy(g, a, d).start()
+
+        @pl.when(self.core != g)
+        def _():
+            self.collect_copy(g, a, 0).start()
+
+        @pl.when(self.core == g)
+        def _():
+            self.last_in[a][self.me[a] * 2 + g] = out[g, self.me[a]]
 
     def collect_wait(self, g, a):
         n = SIZE[a]
         col, width = WIDE[a]
-        sems = self.last_sem[a]
+        sem = self.last_sem[a]
         buf = self.last_in[a]
 
         @pl.when(self.core == g)
         def _():
-            for d in range(n):
-                for c in (g, 1 - g):
-                    if d or c != g:
-                        slot = buf.at[lax.rem(self.me[a] - d + n, n), c]
-                        self.remote(
-                            slot, slot, sems.at[0, g, d], sems.at[1, c, d], self.dev(core=c, **{a: -d})
-                        ).wait_recv()
+            self.settle_all(self.last_out[a].at[g], sem.at[0, g], n - 1)
+            self.settle_all(buf, sem.at[1, 0], 2 * n - 1)
             for c in (0, 1):
-                v = buf[0, c]
+                v = buf[c]
                 for e in range(1, n):
-                    v = v + buf[e, c]
+                    v = v + buf[2 * e + c]
                 self.gh[:, c * HALF + col : c * HALF + col + width] = v.astype(BF16)
 
         @pl.when(self.core != g)
         def _():
-            self.collect_copy(g, a, 0).wait_send()
+            self.settle(self.last_out[a].at[g], sem.at[0, g])
 
     def piece(self, i, y, zl):
         order, _, _ = STREAMS[i]
@@ -288,26 +268,37 @@
 
         @pl.loop(0, NB)
         def _(j):
-            self.weight_copies(j)[1].start()
+            self.weight_copies(j)[1]().start()
 
         for streams, s in ((LONG, 1), (SHORT, 1), (LONG, 2), (LONG, 3), (SHORT, 2), (LONG, 4)):
             for i in streams:
                 self.gather_event(i, 2, s)
 
-    def drain(self, copies):
-        for copy in copies:
-            copy.wait_send()
-
-    def reduce(self, meanwhile):
-        before, self.sends = self.sends, []
+    def settle_ring(self, sems, phases):
+        for i, (order, _, _) in enumerate(STREAMS):
+            for p in phases:
+                ref = self.buf[i].at[0] if p == 1 else self.buf[i]
+                self.settle_all(ref, sems.at[i, p - 1], SIZE[order[p]] - 1)
+
+    def reduce(self):
         for i in LONG + SHORT:
             self.reduce_event(i, 2, 0)
-        for streams, s in ((LONG, 1), (SHORT, 1), (LONG, 2), (LONG, 3)):
-            next(meanwhile, None)
-            if streams is SHORT:
-                self.drain(before)
-            for i in streams:
-                self.reduce_event(i, 2, s)
+        self.grad_weight(0, NB // 2)
+        for i in LONG:
+            self.reduce_event(i, 2, 1)
+        for i in SHORT:
+            self.reduce_event(i, 2, 1)
+        for i in LONG:
+            self.reduce_event(i, 2, 2)
+        self.grad_weight(NB // 2, NB)
+        for i in LONG:
+            self.reduce_event(i, 2, 3)
+        for a in ("z", "y"):
+            self.settle_all(self.first_flat(a), self.first_sem[a].at[0], 2 * SIZE[a] - 1)
+        self.settle_all(self.st0, self.st0_sem.at[0], 15)
+        self.settle_all(self.st1, self.st1_sem.at[0], 7)
+        self.settle(self.lg, self.lg_sem.at[0])
+        self.settle_ring(self.ag_send, (1, 2))
         for i in SHORT:
             self.reduce_event(i, 2, 2)
             self.reduce_event(i, 1, 0)
@@ -322,14 +313,15 @@
             self.collect_send(g, "z")
         for i in LONG:
             self.reduce_event(i, 1, 2)
-        before, self.sends = self.sends, []
         for g in (0, 1):
             self.collect_send(g, "y")
-        self.drain(before)
-        for g in (0, 1):
-            self.collect_wait(g, "z")
-        for g in (0, 1):
-            self.collect_wait(g, "y")
+        self.settle_ring(self.rs_send, (2, 1))
+        half = self.gwb.at[:, pl.ds(0, self.shard)]
+        for e in range(3):
+            self.settle(half, self.g_sem.at[e])
+        for a in ("z", "y"):
+            for g in (0, 1):
+                self.collect_wait(g, a)
 
     def loss_and_grads(self):
         self.wait_weight()
@@ -358,8 +350,7 @@
         top = jnp.max(logits, axis=0, keepdims=True)
         total = jnp.sum(jnp.exp(logits - top), axis=0, keepdims=True)
         picked = jnp.sum(jnp.where(hit, logits, 0.0), axis=0, keepdims=True)
-        merged = self.stats(0, (top, total, picked), [(dx, dy, 0) for dx in range(4) for dy in range(4)])
-        top, total, picked = self.stats(1, merged, [(0, 0, dz) for dz in range(8)])
+        top, total, picked = self.stats(1, self.stats(0, (top, total, picked)))
         lse = top + jnp.log(total)
         self.loss[...] = (lse - picked).reshape(2 * NQ * ROWS)
         dl = scale * (jnp.exp(self.lg_sum[...] - lse) - (row == target).astype(F32))
@@ -376,25 +367,20 @@
                         q = (zh * 4 + x) * 2 * ROWS
                         self.part[i][self.at(order, x, y, zh * ZL + zl)] = o[q : q + 2 * ROWS, off : off + width]
 
-    def stats(self, phase, mine, moves):
+    def stats(self, phase, mine):
         buf = (self.st0, self.st1)[phase]
+        sem = (self.st0_sem, self.st1_sem)[phase]
         own = self.me["x"] * 4 + self.me["y"] if phase == 0 else self.me["z"]
-        sems = (self.st0_sem, self.st1_sem)[phase]
-        pad = jnp.zeros((5, 256), F32)
-        buf[own] = jnp.concatenate(mine + (pad,), axis=0)
-        for e, (dx, dy, dz) in enumerate(moves):
-            if e:
-                self.send(buf.at[own], buf.at[own], sems.at[0, e], sems.at[1, e], self.dev(x=dx, y=dy, z=dz))
-        for e, (dx, dy, dz) in enumerate(moves):
-            if e:
-                if phase == 0:
-                    src = lax.rem(self.me["x"] - dx + 4, 4) * 4 + lax.rem(self.me["y"] - dy + 4, 4)
-                else:
-                    src = lax.rem(self.me["z"] - dz + 8, 8)
-                self.remote(
-                    buf.at[src], buf.at[src], sems.at[0, e], sems.at[1, e], self.dev(x=dx, y=dy, z=dz)
-                ).wait_recv()
-        tiles = [buf[e] for e in range(len(moves))]
+        n = buf.shape[0]
+        buf[own] = jnp.concatenate(mine + (jnp.zeros((5, 256), F32),), axis=0)
+
+        @pl.loop(1, n)
+        def _(e):
+            dev = self.dev(x=e // 4, y=lax.rem(e, 4)) if phase == 0 else self.dev(z=e)
+            self.send(buf.at[own], buf.at[own], sem.at[0], sem.at[1], dev)
+
+        self.settle_all(buf, sem.at[1], n - 1)
+        tiles = [buf[e] for e in range(n)]
         top = tiles[0][0:1]
         for t in tiles[1:]:
             top = jnp.maximum(top, t[0:1])
@@ -408,47 +394,28 @@
         c, other = self.core, 1 - self.core
         rows = pl.ds(pl.multiple_of(c * self.shard, 16), self.shard)
         cols = lambda h: pl.ds(pl.multiple_of(j * FULL + h * HALF, HALF), HALF)
-        theirs = pl.ds(pl.multiple_of(other * self.shard, 16), self.shard)
-        local = pltpu.make_async_copy(self.w.at[:, cols(c)], self.wv.at[j, rows], self.w_sem.at[0, j])
-        out = self.remote(
-            self.w.at[:, cols(other)], self.wv.at[j, rows], self.w_sem.at[1, j], self.w_sem.at[2, j], self.dev(core=other)
+        dst = self.wv.at[j, rows]
+        local = pltpu.make_async_copy(self.w.at[:, cols(c)], dst, self.w_sem.at[0])
+        out = lambda: self.remote(
+            self.w.at[:, cols(other)], dst, self.w_sem.at[1], self.w_sem.at[2], self.dev(core=other)
         )
-        arrive = self.remote(
-            self.w.at[:, cols(other)], self.wv.at[j, theirs], self.w_sem.at[1, j], self.w_sem.at[2, j], self.dev(core=other)
-        )
-        return local, out, arrive
+        return local, out
 
     def wait_weight(self):
-        @pl.loop(0, NB)
-        def _(j):
-            local, out, arrive = self.weight_copies(j)
-            local.wait()
-            out.wait_send()
-            arrive.wait_recv()
-
-    def grad_copies(self, j):
+        half = self.wv.at[:, pl.ds(0, self.shard)]
+        for e in range(3):
+            self.settle(half, self.w_sem.at[e])
+
+    def grad_weight(self, lo, hi):
         c, other = self.core, 1 - self.core
-        cols = lambda h: pl.ds(pl.multiple_of(j * FULL + h * HALF, HALF), HALF)
-        src = lambda h: self.gwb.at[j, pl.ds(pl.multiple_of(h * self.shard, 16), self.shard)]
-        local = pltpu.make_async_copy(src(c), self.gw.at[:, cols(c)], self.g_sem.at[0, j])
-        dev = self.dev(core=other)
-        out = self.remote(src(other), self.gw.at[:, cols(c)], self.g_sem.at[1, j], self.g_sem.at[2, j], dev)
-        arrive = self.remote(src(other), self.gw.at[:, cols(other)], self.g_sem.at[1, j], self.g_sem.at[2, j], dev)
-        return local, out, arrive
-
-    def grad_weight(self, lo, hi):
+
         @pl.loop(lo, hi, unroll=BLOCKS)
         def _(j):
-            o = jnp.dot(self.dlt[...], self.hidden_block(j), preferred_element_type=F32)
-            self.gwb[j] = o.astype(BF16)
-            local, out, _ = self.grad_copies(j)
-            local.start()
-            out.start()
-
-    def grad_quarters(self):
-        for q in range(4):
-            self.grad_weight(q * (NB // 4), (q + 1) * (NB // 4))
-            yield
+            self.gwb[j] = jnp.dot(self.dlt[...], self.hidden_block(j), preferred_element_type=F32).astype(BF16)
+            src = lambda h: self.gwb.at[j, pl.ds(pl.multiple_of(h * self.shard, 16), self.shard)]
+            dst = self.gw.at[:, pl.ds(pl.multiple_of(j * FULL + c * HALF, HALF), HALF)]
+            pltpu.make_async_copy(src(c), dst, self.g_sem.at[0]).start()
+            self.send(src(other), dst, self.g_sem.at[1], self.g_sem.at[2], self.dev(core=other))
 
     def run(self):
         other = 1 - self.core
@@ -460,7 +427,7 @@
         for d in peers:
             pl.semaphore_signal(barrier, inc=1, device_id=self.dev(**d), device_id_type=MESH)
         for a in ("z", "y"):
-            self.spread_copy(a, 0, 0)[0].start()
+            self.spread_own(a).start()
 
         @pl.loop(0, NB)
         def _(j):
@@ -471,16 +438,7 @@
         self.spread_wait()
         self.gather()
         self.loss_and_grads()
-        self.reduce(self.grad_quarters())
-
-        @pl.loop(0, NB)
-        def _(j):
-            local, out, arrive = self.grad_copies(j)
-            local.wait()
-            out.wait_send()
-            arrive.wait_recv()
-
-        self.drain(self.sends)
+        self.reduce()
 
 
 def scratch(shard):
@@ -496,23 +454,23 @@
         "dlt": pltpu.VMEM((rows, 256), BF16),
         "dlr": pltpu.VMEM((256, rows), BF16),
         "gwb": pltpu.VMEM((NB, rows, HALF), BF16),
-        "ag_send": dma((NS, 2, 2, 2, 4)),
+        "ag_send": dma((NS, 2)),
         "ag_recv": dma((NS, 2, 2, 2, 4)),
-        "rs_send": dma((NS, 2, 2, 2, 4)),
+        "rs_send": dma((NS, 2)),
         "rs_recv": dma((NS, 2, 2, 2, 4)),
         "lg_sem": dma((2,)),
-        "st0_sem": dma((2, 16)),
-        "st1_sem": dma((2, 8)),
-        "w_sem": dma((3, NB)),
-        "g_sem": dma((3, NB)),
+        "st0_sem": dma((2,)),
+        "st1_sem": dma((2,)),
+        "w_sem": dma((3,)),
+        "g_sem": dma((3,)),
     }
     for a in ("z", "y"):
         n, width = SIZE[a], WIDE[a][1]
         out[f"first{a}"] = pltpu.VMEM((2, n, ROWS, width), BF16)
-        out[f"first_sem{a}"] = dma((2, 2, n))
+        out[f"first_sem{a}"] = dma((2,))
         out[f"last_out{a}"] = pltpu.VMEM((2, n, ROWS, width), F32)
-        out[f"last_in{a}"] = pltpu.VMEM((n, 2, ROWS, width), F32)
-        out[f"last_sem{a}"] = dma((2, 2, n))
+        out[f"last_in{a}"] = pltpu.VMEM((2 * n, ROWS, width), F32)
+        out[f"last_sem{a}"] = dma((2, 2))
     for i, (order, _, width) in enumerate(STREAMS):
         l, m, f = lead(order)
         out[f"buf{i}"] = pltpu.VMEM((l, m, f, 2 * ROWS, width), BF16)

time: 102 us -> 99.5 us (0.975)
  Pallas kernels: 97.7 us -> 95.1 us
    pallas_call x1, Pallas kernels: 97.7 us -> 95.1 us  [on_device(): pl.pallas_call(body, out_shape=(pltpu.VMEM(loss_weight.shape, F32), pltpu...]
where the time goes in v4:
time: 99.5 us; the launch traced here: 99.4 us
  Pallas kernels  95.1 us (96%)
  local copies, waits for them, and re-layouts  3.71 us (4%)
    pallas_call x1, Pallas kernels, on_device(): pl.pallas_call(body, out_shape=(pltpu.VMEM(loss_weight.shape, F32), pltpu...  95.1 us
    unnamed x3, local copies, waits for them, and re-layouts  3.71 us

profile of v4, /device:TPU:1, one launch (start us, length us, event | category | flops | bytes accessed | tf_op | source)
XLA Modules:
  0.0 99.4 jit_solution(10214137324306308201)
XLA Ops:
  0.6 95.1 %shard_map.67 = (f32[256]{0:T(256)S(1)}, bf16[176,16384]{1,0:T(8,128)(2,1)S(1)}, bf16[16,1024]{1,0:T(8,128)(2,1)S(1)}) custom-call(bf16[16,1024]{1,0:T(8,128)(2,1)} %hid.1, bf16[176,16384]{1,0:T(8,128)(2,1)} %w.1, s32[256]{0:T(256)} %tgt.1, f32[256]{0:T(256)} %lw.1), custom_call_target="tpu_custom_call" | custom-call | flops 4429185024 | bytes 11534336 | tf_op jit(solution)/shard_map/pallas_call | solution.py:503
  95.7 0.6 copy.10
  96.3 0.6 copy.12
  96.9 2.5 %copy.11 = bf16[176,16384]{1,0:T(8,128)(2,1)} copy(bf16[176,16384]{1,0:T(8,128)(2,1)S(1)} %get-tuple-element.4) | data formatting | bytes 11534336

commit v5 on v4

--- a/solution.py
+++ b/solution.py
@@ -17,13 +17,10 @@
 FULL, HALF = 1024, 512
 STREAMS = (
     (("z", "b", "a"), 0, 256),
-    (("z", "a", "b"), 256, 128),
-    (("y", "x", "z"), 384, 128),
+    (("z", "a", "b"), 256, 256),
 )
 NS = len(STREAMS)
-WIDE = {"z": (0, 384), "y": (384, 128)}
-LONG = [i for i in range(NS) if STREAMS[i][0][2] == "z"]
-SHORT = [i for i in range(NS) if i not in LONG]
+WIDE = {"z": (0, 512)}
 BLOCKS = 2
 
 
@@ -86,7 +83,7 @@
         return pltpu.make_async_copy(src, self.first[a].at[self.core, self.me[a]], self.first_sem[a].at[1])
 
     def spread(self):
-        for a in ("z", "y"):
+        for a in WIDE:
             n = SIZE[a]
             col, width = WIDE[a]
 
@@ -102,7 +99,7 @@
         return self.first[a].reshape(2 * SIZE[a], ROWS, WIDE[a][1])
 
     def spread_wait(self):
-        for a in ("z", "y"):
+        for a in WIDE:
             self.settle(self.first[a], self.first_sem[a].at[1])
 
     def settle_all(self, ref, sem, count):
@@ -262,7 +259,7 @@
             self.gather_event(i, 1, 0)
         for i in range(NS):
             self.gather_event(i, 1, 1)
-        for i in LONG + SHORT:
+        for i in range(NS):
             self.gather_event(i, 1, 2)
             self.gather_event(i, 2, 0)
 
@@ -270,8 +267,8 @@
         def _(j):
             self.weight_copies(j)[1]().start()
 
-        for streams, s in ((LONG, 1), (SHORT, 1), (LONG, 2), (LONG, 3), (SHORT, 2), (LONG, 4)):
-            for i in streams:
+        for s in (1, 2):
+            for i in range(NS):
                 self.gather_event(i, 2, s)
 
     def settle_ring(self, sems, phases):
@@ -281,47 +278,31 @@
                 self.settle_all(ref, sems.at[i, p - 1], SIZE[order[p]] - 1)
 
     def reduce(self):
-        for i in LONG + SHORT:
+        for i in range(NS):
             self.reduce_event(i, 2, 0)
         self.grad_weight(0, NB // 2)
-        for i in LONG:
+        for i in range(NS):
             self.reduce_event(i, 2, 1)
-        for i in SHORT:
-            self.reduce_event(i, 2, 1)
-        for i in LONG:
-            self.reduce_event(i, 2, 2)
         self.grad_weight(NB // 2, NB)
-        for i in LONG:
-            self.reduce_event(i, 2, 3)
-        for a in ("z", "y"):
-            self.settle_all(self.first_flat(a), self.first_sem[a].at[0], 2 * SIZE[a] - 1)
+        self.settle_all(self.first_flat("z"), self.first_sem["z"].at[0], 2 * SIZE["z"] - 1)
         self.settle_all(self.st0, self.st0_sem.at[0], 15)
         self.settle_all(self.st1, self.st1_sem.at[0], 7)
         self.settle(self.lg, self.lg_sem.at[0])
         self.settle_ring(self.ag_send, (1, 2))
-        for i in SHORT:
+        for i in range(NS):
             self.reduce_event(i, 2, 2)
             self.reduce_event(i, 1, 0)
-        for i in LONG:
-            self.reduce_event(i, 2, 4)
-            self.reduce_event(i, 1, 0)
-        for i in SHORT + LONG:
-            self.reduce_event(i, 1, 1)
-        for i in SHORT:
-            self.reduce_event(i, 1, 2)
+        for s in (1, 2):
+            for i in range(NS):
+                self.reduce_event(i, 1, s)
         for g in (0, 1):
             self.collect_send(g, "z")
-        for i in LONG:
-            self.reduce_event(i, 1, 2)
-        for g in (0, 1):
-            self.collect_send(g, "y")
         self.settle_ring(self.rs_send, (2, 1))
         half = self.gwb.at[:, pl.ds(0, self.shard)]
         for e in range(3):
             self.settle(half, self.g_sem.at[e])
-        for a in ("z", "y"):
-            for g in (0, 1):
-                self.collect_wait(g, a)
+        for g in (0, 1):
+            self.collect_wait(g, "z")
 
     def loss_and_grads(self):
         self.wait_weight()
@@ -423,10 +404,9 @@
         peers = [dict(x=dx, y=dy) for dx in range(4) for dy in range(4) if dx or dy]
         peers += [dict(z=dz) for dz in range(1, 8)]
         peers += [dict(core=other, z=dz) for dz in range(8)]
-        peers += [dict(core=other, y=dy) for dy in range(1, 4)]
         for d in peers:
             pl.semaphore_signal(barrier, inc=1, device_id=self.dev(**d), device_id_type=MESH)
-        for a in ("z", "y"):
+        for a in WIDE:
             self.spread_own(a).start()
 
         @pl.loop(0, NB)
@@ -464,7 +444,7 @@
         "w_sem": dma((3,)),
         "g_sem": dma((3,)),
     }
-    for a in ("z", "y"):
+    for a in WIDE:
         n, width = SIZE[a], WIDE[a][1]
         out[f"first{a}"] = pltpu.VMEM((2, n, ROWS, width), BF16)
         out[f"first_sem{a}"] = dma((2,))
@@ -495,7 +475,7 @@
         for kind in ("rs_out", "rs_in"):
             args[kind] = [{p: named.pop(f"{kind}{i}{p}") for p in (1, 2)} for i in range(NS)]
         for kind in ("first", "first_sem", "last_out", "last_in", "last_sem"):
-            args[kind] = {a: named.pop(f"{kind}{a}") for a in ("z", "y")}
+            args[kind] = {a: named.pop(f"{kind}{a}") for a in WIDE}
         args.update(named)
         Kernel(shard, args).run()
 

time: 99.5 us -> 109 us (1.095)
  Pallas kernels: 95.1 us -> 105 us
    pallas_call x1, Pallas kernels: 95.1 us -> 105 us  [on_device(): pl.pallas_call(body, out_shape=(pltpu.VMEM(loss_weight.shape, F32), pltpu...]
where the time goes in v5:
time: 109 us
  Pallas kernels  105 us (96%)
  local copies, waits for them, and re-layouts  3.71 us (3%)
    pallas_call x1, Pallas kernels, on_device(): pl.pallas_call(body, out_shape=(pltpu.VMEM(loss_weight.shape, F32), pltpu...  105 us
    unnamed x3, local copies, waits for them, and re-layouts  3.71 us

profile of v5, /device:TPU:1, one launch (start us, length us, event | category | flops | bytes accessed | tf_op | source)
XLA Modules:
  0.0 109.0 jit_solution(17424028645205139761)
XLA Ops:
  0.6 104.6 %shard_map.67 = (f32[256]{0:T(256)S(1)}, bf16[176,16384]{1,0:T(8,128)(2,1)S(1)}, bf16[16,1024]{1,0:T(8,128)(2,1)S(1)}) custom-call(bf16[16,1024]{1,0:T(8,128)(2,1)} %hid.1, bf16[176,16384]{1,0:T(8,128)(2,1)} %w.1, s32[256]{0:T(256)} %tgt.1, f32[256]{0:T(256)} %lw.1), custom_call_target="tpu_custom_call" | custom-call | flops 4429185024 | bytes 11534336 | tf_op jit(solution)/shard_map/pallas_call | solution.py:483
  105.3 0.6 copy.10
  105.8 0.6 copy.12
  106.5 2.5 %copy.11 = bf16[176,16384]{1,0:T(8,128)(2,1)} copy(bf16[176,16384]{1,0:T(8,128)(2,1)S(1)} %get-tuple-element.4) | data formatting | bytes 11534336

commit v6 on v4

--- a/solution.py
+++ b/solution.py
@@ -16,12 +16,12 @@
 ROWS = 16
 FULL, HALF = 1024, 512
 STREAMS = (
-    (("z", "b", "a"), 0, 256),
-    (("z", "a", "b"), 256, 128),
-    (("y", "x", "z"), 384, 128),
+    (("z", "b", "a"), 0, 128),
+    (("z", "a", "b"), 128, 128),
+    (("y", "x", "z"), 256, 256),
 )
 NS = len(STREAMS)
-WIDE = {"z": (0, 384), "y": (384, 128)}
+WIDE = {"z": (0, 256), "y": (256, 256)}
 LONG = [i for i in range(NS) if STREAMS[i][0][2] == "z"]
 SHORT = [i for i in range(NS) if i not in LONG]
 BLOCKS = 2

time: 99.5 us -> 104 us (1.045)
  Pallas kernels: 95.1 us -> 100 us
    pallas_call x1, Pallas kernels: 95.1 us -> 100 us  [on_device(): pl.pallas_call(body, out_shape=(pltpu.VMEM(loss_weight.shape, F32), pltpu...]
where the time goes in v6:
time: 104 us
  Pallas kernels  100 us (96%)
  local copies, waits for them, and re-layouts  3.71 us (4%)
    pallas_call x1, Pallas kernels, on_device(): pl.pallas_call(body, out_shape=(pltpu.VMEM(loss_weight.shape, F32), pltpu...  100 us
    unnamed x3, local copies, waits for them, and re-layouts  3.71 us

profile of v6, /device:TPU:1, one launch (start us, length us, event | category | flops | bytes accessed | tf_op | source)
XLA Modules:
  0.0 104.4 jit_solution(9125870338752294845)
XLA Ops:
  0.6 100.0 %shard_map.67 = (f32[256]{0:T(256)S(1)}, bf16[176,16384]{1,0:T(8,128)(2,1)S(1)}, bf16[16,1024]{1,0:T(8,128)(2,1)S(1)}) custom-call(bf16[16,1024]{1,0:T(8,128)(2,1)} %hid.1, bf16[176,16384]{1,0:T(8,128)(2,1)} %w.1, s32[256]{0:T(256)} %tgt.1, f32[256]{0:T(256)} %lw.1), custom_call_target="tpu_custom_call" | custom-call | flops 4429185024 | bytes 11534336 | tf_op jit(solution)/shard_map/pallas_call | solution.py:503
  100.6 0.6 copy.10
  101.2 0.6 copy.12
  101.8 2.5 %copy.11 = bf16[176,16384]{1,0:T(8,128)(2,1)} copy(bf16[176,16384]{1,0:T(8,128)(2,1)S(1)} %get-tuple-element.4) | data formatting | bytes 11534336

commit v7 on v4

--- a/solution.py
+++ b/solution.py
@@ -262,7 +262,7 @@
             self.gather_event(i, 1, 0)
         for i in range(NS):
             self.gather_event(i, 1, 1)
-        for i in LONG + SHORT:
+        for i in SHORT + LONG:
             self.gather_event(i, 1, 2)
             self.gather_event(i, 2, 0)
 
@@ -281,18 +281,20 @@
                 self.settle_all(ref, sems.at[i, p - 1], SIZE[order[p]] - 1)
 
     def reduce(self):
-        for i in LONG + SHORT:
+        quarter = NB // 4
+        for i in SHORT + LONG:
             self.reduce_event(i, 2, 0)
-        self.grad_weight(0, NB // 2)
         for i in LONG:
             self.reduce_event(i, 2, 1)
+        self.grad_weight(0, quarter)
         for i in SHORT:
             self.reduce_event(i, 2, 1)
         for i in LONG:
             self.reduce_event(i, 2, 2)
-        self.grad_weight(NB // 2, NB)
+        self.grad_weight(quarter, 2 * quarter)
         for i in LONG:
             self.reduce_event(i, 2, 3)
+        self.grad_weight(2 * quarter, NB)
         for a in ("z", "y"):
             self.settle_all(self.first_flat(a), self.first_sem[a].at[0], 2 * SIZE[a] - 1)
         self.settle_all(self.st0, self.st0_sem.at[0], 15)

time: 99.5 us -> 98.8 us (level)
  no operation moved by 1% of the time
where the time goes in v7:
time: 98.8 us; the launch traced here: 98.7 us
  Pallas kernels  94.4 us (96%)
  local copies, waits for them, and re-layouts  3.71 us (4%)
    pallas_call x1, Pallas kernels, on_device(): pl.pallas_call(body, out_shape=(pltpu.VMEM(loss_weight.shape, F32), pltpu...  94.4 us
    unnamed x3, local copies, waits for them, and re-layouts  3.71 us

profile of v7, /device:TPU:1, one launch (start us, length us, event | category | flops | bytes accessed | tf_op | source)
XLA Modules:
  0.0 98.7 jit_solution(9026461593766663210)
XLA Ops:
  0.6 94.4 %shard_map.67 = (f32[256]{0:T(256)S(1)}, bf16[176,16384]{1,0:T(8,128)(2,1)S(1)}, bf16[16,1024]{1,0:T(8,128)(2,1)S(1)}) custom-call(bf16[16,1024]{1,0:T(8,128)(2,1)} %hid.1, bf16[176,16384]{1,0:T(8,128)(2,1)} %w.1, s32[256]{0:T(256)} %tgt.1, f32[256]{0:T(256)} %lw.1), custom_call_target="tpu_custom_call" | custom-call | flops 4429185024 | bytes 11534336 | tf_op jit(solution)/shard_map/pallas_call | solution.py:505
  95.0 0.6 copy.10
  95.6 0.6 copy.12
  96.2 2.5 %copy.11 = bf16[176,16384]{1,0:T(8,128)(2,1)} copy(bf16[176,16384]{1,0:T(8,128)(2,1)S(1)} %get-tuple-element.4) | data formatting | bytes 11534336

commit v8 on v7

--- a/solution.py
+++ b/solution.py
@@ -265,14 +265,15 @@
         for i in SHORT + LONG:
             self.gather_event(i, 1, 2)
             self.gather_event(i, 2, 0)
-
-        @pl.loop(0, NB)
-        def _(j):
-            self.weight_copies(j)[1]().start()
-
         for streams, s in ((LONG, 1), (SHORT, 1), (LONG, 2), (LONG, 3), (SHORT, 2), (LONG, 4)):
             for i in streams:
                 self.gather_event(i, 2, s)
+            if streams is SHORT and s == 1:
+
+                @pl.loop(0, NB)
+                def _(j):
+                    self.weight_copies(j)[1]().start()
+
 
     def settle_ring(self, sems, phases):
         for i, (order, _, _) in enumerate(STREAMS):

time: 98.8 us -> 99.4 us (level)
  no operation moved by 1% of the time
where the time goes in v8:
time: 99.4 us; the launch traced here: 99.3 us
  Pallas kernels  94.9 us (95%)
  local copies, waits for them, and re-layouts  3.71 us (4%)
    pallas_call x1, Pallas kernels, on_device(): pl.pallas_call(body, out_shape=(pltpu.VMEM(loss_weight.shape, F32), pltpu...  94.9 us
    unnamed x3, local copies, waits for them, and re-layouts  3.71 us

profile of v8, /device:TPU:1, one launch (start us, length us, event | category | flops | bytes accessed | tf_op | source)
XLA Modules:
  0.0 99.3 jit_solution(3957604398308803134)
XLA Ops:
  0.6 94.9 %shard_map.67 = (f32[256]{0:T(256)S(1)}, bf16[176,16384]{1,0:T(8,128)(2,1)S(1)}, bf16[16,1024]{1,0:T(8,128)(2,1)S(1)}) custom-call(bf16[16,1024]{1,0:T(8,128)(2,1)} %hid.1, bf16[176,16384]{1,0:T(8,128)(2,1)} %w.1, s32[256]{0:T(256)} %tgt.1, f32[256]{0:T(256)} %lw.1), custom_call_target="tpu_custom_call" | custom-call | flops 4429185024 | bytes 11534336 | tf_op jit(solution)/shard_map/pallas_call | solution.py:506
  95.6 0.6 copy.10
  96.2 0.6 copy.12
  96.8 2.5 %copy.11 = bf16[176,16384]{1,0:T(8,128)(2,1)} copy(bf16[176,16384]{1,0:T(8,128)(2,1)S(1)} %get-tuple-element.4) | data formatting | bytes 11534336
